TPU v7x, 128 devices: a whole 4x4x4 slice. The times are simulated.
128 devices in a mesh: segment: 2 (over x_lo), seq: 16 (over x_hi, y, core), head: 4 (over z).
Axes of the slice: x: 4 (x_hi: 2, x_lo: 2; x = x_hi * 2 + x_lo), y: 4, z: 4, core: 2. Of those that a mesh axis runs over, the one named last changes fastest.
Arguments:
- stream: bfloat16 [2, 2048, 4096], P(None, 'seq', 'head'), may hold values from -6 to 6
- in_gain: float32 [2, 4096], P('segment'), may hold values from 0.25 to 1.75
- w_qkv: bfloat16 [2, 4096, 4, 3, 512], P('segment', None, 'head'), may hold values from -0.09375 to 0.09375
- qk_gain: float32 [2, 4, 2, 512], P('segment', 'head'), may hold values from 0.25 to 1.75
- w_one: bfloat16 [2, 4, 512, 768], P('segment', 'head'), may hold values from -0.25 to 0.25
- w_three: bfloat16 [2, 4, 512, 768], P('segment', 'head'), may hold values from -0.25 to 0.25
- w_two: bfloat16 [2, 4, 768, 512], P('segment', 'head'), may hold values from -0.21875 to 0.21875
- token_rate: float32 [2, 2, 2048], P('segment', None, 'seq'), may hold values from 0.05 to 1
- out_gain: float32 [2, 4, 512], P('segment', 'head'), may hold values from 0.25 to 1.75
- w_out: bfloat16 [2, 4, 512, 4096], P('segment', 'head'), may hold values from -0.125 to 0.125
Outputs:
- sections_out: bfloat16 [2, 2, 2048, 4096], P('segment', None, 'seq', 'head')
All inputs are finite; a program needn't handle non-finite values.
Results may differ from a plain program's by a relative error of at most 0.038.
Values may be sent and summed in bfloat16 or wider, within the bound.
No kernel may reach another device: no remote copies, remote signals or barrier semaphores. Data moves between devices by JAX's collectives and lax.ppermute only.
A program may use at most 128 MiB of HBM per device.

v0:
```python
import jax
import jax.numpy as jnp
from jax import lax
from jax.sharding import Mesh
from jax.sharding import PartitionSpec as P

NS_STEPS = 2
SEQ = ("seq_0", "seq_1", "seq_2")


ns_first = 3.4445
ns_second = -4.775
ns_third = 2.0315
update_step = 1.0
norm_eps = 1e-06
grad_eps = 1e-07


def from_everyone(array, axis):
    copies = jnp.broadcast_to(array, (lax.axis_size(axis), *array.shape))
    return lax.all_to_all(copies, axis, split_axis=0, concat_axis=0, tiled=True)


def taken_together(array, axis):
    everything = from_everyone(array, axis)
    return jnp.sum(everything, axis=0)


def filled_up(lines, devices):
    spare = -len(lines) % devices
    return jnp.pad(lines, [(0, spare)] + [(0, 0)] * (lines.ndim - 1))


def joined_along(pieces, dim):
    dims = list(pieces.shape[1:])
    dims[dim] *= pieces.shape[0]
    return jnp.moveaxis(pieces, 0, dim).reshape(dims)


def gather_axes(array, axes, dim):
    far, near = axes
    pieces = from_everyone(from_everyone(array, far), near)
    return joined_along(pieces.swapaxes(0, 1).reshape(-1, *array.shape), dim)


def in_blocks(array, dim, devices):
    dims = array.shape
    pieces = array.reshape(*dims[:dim], devices, dims[dim] // devices, *dims[dim + 1 :])
    return jnp.moveaxis(pieces, dim, 0)


def summed_on_arrival(array, axis, dim):
    devices = lax.axis_size(axis)
    pieces = lax.all_to_all(in_blocks(array, dim, devices), axis, 0, 0, tiled=True)
    return jnp.sum(pieces.astype(jnp.float32), axis=0)


def sum_by_axis(array, axes, dim):
    far, near = axes
    own = summed_on_arrival(in_blocks(array, dim, lax.axis_size(far)), near, dim + 1)
    return jnp.sum(
        lax.all_to_all(own.astype(jnp.bfloat16), far, 0, 0, tiled=True).astype(jnp.float32), axis=0
    )


def sum_by_parts(array, axes):
    lines = array.reshape(-1, array.shape[-1])
    padded = filled_up(lines, lax.axis_size(axes[0]) * lax.axis_size(axes[1]))
    whole = gather_axes(sum_by_axis(padded, axes, 0).astype(jnp.bfloat16), axes, 0)
    return lax.slice_in_dim(whole, 0, len(lines)).reshape(array.shape).astype(jnp.float32)


def gather_turned(arrays, axis, dims):
    turned = [jnp.moveaxis(a, dim, 0) for a, dim in zip(arrays, dims)]
    widths = [t[0].size for t in turned]
    both = jnp.concatenate([t.reshape(-1, w) for t, w in zip(turned, widths)], axis=1)
    whole = lax.all_gather(both, axis, axis=0, tiled=True)
    pieces = jnp.split(whole, [sum(widths[:k]) for k in range(1, len(widths))], axis=1)
    return tuple(
        (
            jnp.moveaxis(b.reshape(-1, *t.shape[1:]), 0, dim)
            for b, t, dim in zip(pieces, turned, dims)
        )
    )


def gathered_copies(array, axis, dim):
    return joined_along(from_everyone(array, axis), dim)


def in_one_piece(arrays, axis, dim, along):
    ends, at = ([], 0)
    for a in arrays[:-1]:
        at += a.shape[along]
        ends.append(at)
    both = jnp.concatenate(arrays, axis=along)
    return tuple(jnp.split(sum_by_axis(both, axis, dim), ends, axis=along))


def shifted(array, axis, by):
    devices = lax.axis_size(axis)
    pairs = [(i, i + by) for i in range(devices) if 0 <= i + by < devices]
    return lax.ppermute(array, axis, pairs)


def rms_scale(values):
    return values * lax.rsqrt(jnp.mean(values * values, axis=-1, keepdims=True) + norm_eps)


def contract_rows(left, right):
    return lax.dot_general(
        left, right, (((0,), (0,)), ((), ())), preferred_element_type=jnp.float32
    )


def renormalize(weights, target_norms):
    return weights * (target_norms / (jnp.sqrt(jnp.sum(weights * weights, axis=0)) + norm_eps))


def orthogonal_updates(shares):
    squares = jnp.stack([jnp.sum(share * share) for share in shares])
    totals = taken_together(squares, SEQ)
    current = [
        (shares[index] / (jnp.sqrt(totals[index]) + grad_eps)).astype(jnp.bfloat16)
        for index in range(3)
    ]
    for sweep_index in range(NS_STEPS):
        partial_grams = jnp.stack(
            [
                lax.dot_general(
                    block, block, (((1,), (1,)), ((), ())), preferred_element_type=jnp.float32
                )
                .astype(jnp.bfloat16)
                .astype(jnp.float32)
                for block in current
            ]
        )
        grams = sum_by_parts(
            partial_grams.astype(jnp.bfloat16), (("seq_0", "seq_1"), "seq_2")
        ).astype(jnp.bfloat16)
        following = []
        for index in range(3):
            gram_matrix = grams[index]
            square = jnp.dot(gram_matrix, gram_matrix, preferred_element_type=jnp.float32)
            mixing = (ns_second * gram_matrix.astype(jnp.float32) + ns_third * square).astype(
                jnp.bfloat16
            )
            block = current[index]
            following.append(
                (
                    ns_first * block.astype(jnp.float32)
                    + jnp.dot(mixing, block, preferred_element_type=jnp.float32)
                ).astype(jnp.bfloat16)
            )
        current = following
    return gather_turned((current[0], current[1], current[2]), SEQ, (1, 1, 1))


def run_section(
    residual, gain_row, qkv_matrix, head_gains, rate_row, out_gain_row, out_weights, fasts, norms
):
    values = residual.astype(jnp.float32)
    head_width = head_gains.shape[-1]
    whole = gathered_copies(residual, "head", 1)
    normed = (rms_scale(whole.astype(jnp.float32)) * gain_row).astype(jnp.bfloat16)
    projected = jnp.dot(normed, qkv_matrix, preferred_element_type=jnp.float32)
    projected = projected.reshape(residual.shape[0], 3, head_width)
    queries = rms_scale(projected[:, 0]) * head_gains[0]
    key_rows = (rms_scale(projected[:, 1]) * head_gains[1]).astype(jnp.bfloat16)
    out_grad = (-rate_row[:, None] * projected[:, 2]).astype(jnp.bfloat16)
    gate_fast, up_fast, down_fast = fasts
    gate_low = gate_fast.astype(jnp.bfloat16)
    up_low = up_fast.astype(jnp.bfloat16)
    down_low = down_fast.astype(jnp.bfloat16)
    pre_gate = jnp.dot(key_rows, gate_low, preferred_element_type=jnp.float32)
    pre_up = jnp.dot(key_rows, up_low, preferred_element_type=jnp.float32)
    sigmoid_gate = jax.nn.sigmoid(pre_gate)
    gated = pre_gate * sigmoid_gate
    hidden = (gated * pre_up).astype(jnp.bfloat16)
    backward = lax.dot_general(
        out_grad, down_low, (((1,), (1,)), ((), ())), preferred_element_type=jnp.float32
    )
    grad_gate = (backward * pre_up * sigmoid_gate * (1.0 + pre_gate * (1.0 - sigmoid_gate))).astype(
        jnp.bfloat16
    )
    grad_up = (backward * gated).astype(jnp.bfloat16)
    shares = in_one_piece(
        (
            contract_rows(key_rows, grad_gate).astype(jnp.bfloat16),
            contract_rows(key_rows, grad_up).astype(jnp.bfloat16),
            contract_rows(out_grad, hidden).astype(jnp.bfloat16),
        ),
        (("seq_0", "seq_1"), "seq_2"),
        1,
        0,
    )
    gate_step, up_step, down_step = orthogonal_updates(shares)
    gate_fast = renormalize(gate_fast - update_step * gate_step.astype(jnp.float32), norms[0])
    up_fast = renormalize(up_fast - update_step * up_step.astype(jnp.float32), norms[1])
    down_fast = renormalize(down_fast - update_step * down_step.astype(jnp.float32).T, norms[2])
    gate_out = jnp.dot(queries, gate_fast, precision=lax.Precision.HIGHEST)
    up_out = jnp.dot(queries, up_fast, precision=lax.Precision.HIGHEST)
    output = jnp.dot(jax.nn.silu(gate_out) * up_out, down_fast, precision=lax.Precision.HIGHEST)
    normed_out = (rms_scale(output) * out_gain_row).astype(jnp.bfloat16)
    head_terms = jnp.dot(normed_out, out_weights, preferred_element_type=jnp.float32)
    delta = summed_on_arrival(head_terms.astype(jnp.bfloat16), "head", 1)
    return ((values + delta).astype(jnp.bfloat16), (gate_fast, up_fast, down_fast))


def shards(stream, in_gain, w_qkv, qk_gain, w_one, w_three, w_two, token_rate, out_gain, w_out):
    segment_index = lax.axis_index("segment")
    span_count = stream.shape[0]
    moments = span_count + lax.axis_size("segment") - 1
    qkv_matrix = w_qkv[0].reshape(w_qkv.shape[1], -1)
    fasts = (
        w_one[0, 0].astype(jnp.float32),
        w_three[0, 0].astype(jnp.float32),
        w_two[0, 0].astype(jnp.float32),
    )
    norms = tuple((jnp.sqrt(jnp.sum(matrix * matrix, axis=0)) for matrix in fasts))
    received = jnp.zeros_like(stream[0])
    collected = jnp.zeros(stream.shape, jnp.bfloat16)
    for moment in range(moments):
        span_index = moment - segment_index
        active = (span_index >= 0) & (span_index < span_count)
        clipped = jnp.clip(span_index, 0, span_count - 1)
        source = jnp.where(segment_index == 0, stream[min(moment, span_count - 1)], received)
        rate_row = lax.dynamic_index_in_dim(token_rate[0], clipped, 0, keepdims=False)
        result, updated = run_section(
            source,
            in_gain[0],
            qkv_matrix,
            qk_gain[0, 0],
            rate_row,
            out_gain[0, 0],
            w_out[0, 0],
            fasts,
            norms,
        )
        fasts = tuple((jnp.where(active, fresh, former) for fresh, former in zip(updated, fasts)))
        chosen = jnp.arange(span_count) == span_index
        collected = jnp.where(chosen[:, None, None], result[None], collected)
        if moment + 1 < moments:
            received = shifted(result, "segment", 1)
    return collected[None]


def solution(mesh):
    torus = Mesh(
        mesh.devices.reshape(mesh.shape["segment"], 2, 4, 2, mesh.shape["head"]),
        ("segment", "seq_0", "seq_1", "seq_2", "head"),
    )
    return jax.shard_map(
        shards,
        mesh=torus,
        in_specs=(
            P(None, SEQ, "head"),
            P("segment", None),
            P("segment", None, "head", None, None),
            P("segment", "head", None, None),
            P("segment", "head", None, None),
            P("segment", "head", None, None),
            P("segment", "head", None, None),
            P("segment", None, SEQ),
            P("segment", "head", None),
            P("segment", "head", None, None),
        ),
        out_specs=P("segment", None, SEQ, "head"),
        check_vma=False,
    )
```

profile of v0, /device:TPU:1, one launch (start us, length us, event | category | flops | bytes accessed | tf_op | source)
XLA Modules:
  0.0 894.6 jit_solution(10123162408397676524)
XLA Ops:
  15.8 16.9 %copy.149 = bf16[1,4096,1,3,512]{1,4,3,2,0:T(8,128)(2,1)} copy(bf16[1,4096,1,3,512]{4,1,3,2,0:T(8,128)(2,1)} %param.12) | data formatting | bytes 25165824 | tf_op args[2]
  61.0 24.3 %all_to_all.199 = bf16[8,1536,48]{1,2,0:T(8,128)(2,1)S(1)} all-to-all(bf16[8,1536,48]{1,2,0:T(8,128)(2,1)} %reduce_sum.563), channel_id=1, replica_groups=mesh['segment'=2,'seq_0'=2,'seq_1'=4,'seq_2'=2,'head'=4] {'seq_0','seq_1'}, dimensions={0} | all-to-all | bytes 2359296 | tf_op jit(solution)/shard_map/all_to_all | solution.py:62
  109.7 15.6 %all_to_all.202 = bf16[8,96,512]{2,1,0:T(8,128)(2,1)S(1)} all-to-all(bf16[8,96,512]{2,1,0:T(8,128)(2,1)S(1)} %reduce_sum.569), channel_id=1, replica_groups=mesh['segment'=2,'seq_0'=2,'seq_1'=4,'seq_2'=2,'head'=4] {'seq_0','seq_1'}, dimensions={0} | all-to-all | bytes 1572864 | tf_op jit(solution)/shard_map/all_to_all | solution.py:62
  125.5 16.8 %all_to_all.203 = bf16[8,96,512]{2,1,0:T(8,128)(2,1)S(1)} all-to-all(bf16[8,96,512]{2,1,0:T(8,128)(2,1)S(1)} %broadcast_in_dim.133), channel_id=1, replica_groups=mesh['segment'=2,'seq_0'=2,'seq_1'=4,'seq_2'=2,'head'=4] {'seq_0','seq_1'}, dimensions={0} | all-to-all | bytes 1572864 | tf_op jit(solution)/shard_map/all_to_all | solution.py:21
  158.7 15.4 %all_to_all.206 = bf16[8,96,512]{2,1,0:T(8,128)(2,1)S(1)} all-to-all(bf16[8,96,512]{2,1,0:T(8,128)(2,1)S(1)} %reduce_sum.571), channel_id=1, replica_groups=mesh['segment'=2,'seq_0'=2,'seq_1'=4,'seq_2'=2,'head'=4] {'seq_0','seq_1'}, dimensions={0} | all-to-all | bytes 1572864 | tf_op jit(solution)/shard_map/all_to_all | solution.py:62
  174.3 16.7 %all_to_all.207 = bf16[8,96,512]{2,1,0:T(8,128)(2,1)S(1)} all-to-all(bf16[8,96,512]{2,1,0:T(8,128)(2,1)S(1)} %broadcast_in_dim.135), channel_id=1, replica_groups=mesh['segment'=2,'seq_0'=2,'seq_1'=4,'seq_2'=2,'head'=4] {'seq_0','seq_1'}, dimensions={0} | all-to-all | bytes 1572864 | tf_op jit(solution)/shard_map/all_to_all | solution.py:21
  203.7 43.8 %all-gather.4.cloned.1.call-done = bf16[768,1536]{1,0:T(8,128)(2,1)} async-done(((bf16[48,1536]{1,0:T(8,128)(2,1)}), bf16[768,1536]{1,0:T(8,128)(2,1)}) %all-gather.4.cloned.1.call-update) | async-done | bytes 2359312 | tf_op jit(solution)/shard_map/all_gather | solution.py:77
  258.2 18.7 %all_to_all.209 = bf16[4,128,1024]{2,1,0:T(8,128)(2,1)S(1)} all-to-all(bf16[4,128,1024]{2,1,0:T(8,128)(2,1)S(1)} %bitcast.671), channel_id=1, replica_groups=mesh['segment'=2,'seq_0'=2,'seq_1'=4,'seq_2'=2,'head'=4] {'head'}, dimensions={0} | all-to-all | bytes 2097152 | tf_op jit(solution)/shard_map/all_to_all | solution.py:54
  290.6 12.5 %all-to-all-done.13 = bf16[4,128,1024]{2,1,0:T(8,128)(2,1)} async-done(((bf16[4,128,1024]{2,1,0:T(8,128)(2,1)}), bf16[4,128,1024]{2,1,0:T(8,128)(2,1)}, u32[]{:S(2)}, u32[]{:S(2)}) %all-to-all-start.13) | async-done | bytes 1048608 | tf_op jit(solution)/shard_map/all_to_all | solution.py:21
  342.5 22.6 %all_to_all.211 = bf16[8,1536,48]{1,2,0:T(8,128)(2,1)S(1)} all-to-all(bf16[8,1536,48]{1,2,0:T(8,128)(2,1)} %reduce_sum.584), channel_id=1, replica_groups=mesh['segment'=2,'seq_0'=2,'seq_1'=4,'seq_2'=2,'head'=4] {'seq_0','seq_1'}, dimensions={0} | all-to-all | bytes 2359296 | tf_op jit(solution)/shard_map/all_to_all | solution.py:62
  392.1 17.4 %all_to_all.214 = bf16[8,96,512]{2,1,0:T(8,128)(2,1)} all-to-all(bf16[8,96,512]{2,1,0:T(8,128)(2,1)} %reduce_sum.590), channel_id=1, replica_groups=mesh['segment'=2,'seq_0'=2,'seq_1'=4,'seq_2'=2,'head'=4] {'seq_0','seq_1'}, dimensions={0} | all-to-all | bytes 1572864 | tf_op jit(solution)/shard_map/all_to_all | solution.py:62
  410.7 16.8 %all_to_all.215 = bf16[8,96,512]{2,1,0:T(8,128)(2,1)S(1)} all-to-all(bf16[8,96,512]{2,1,0:T(8,128)(2,1)S(1)} %broadcast_in_dim.139), channel_id=1, replica_groups=mesh['segment'=2,'seq_0'=2,'seq_1'=4,'seq_2'=2,'head'=4] {'seq_0','seq_1'}, dimensions={0} | all-to-all | bytes 1572864 | tf_op jit(solution)/shard_map/all_to_all | solution.py:21
  454.2 17.4 %all_to_all.218 = bf16[8,96,512]{2,1,0:T(8,128)(2,1)} all-to-all(bf16[8,96,512]{2,1,0:T(8,128)(2,1)} %reduce_sum.592), channel_id=1, replica_groups=mesh['segment'=2,'seq_0'=2,'seq_1'=4,'seq_2'=2,'head'=4] {'seq_0','seq_1'}, dimensions={0} | all-to-all | bytes 1572864 | tf_op jit(solution)/shard_map/all_to_all | solution.py:62
  472.8 16.8 %all_to_all.219 = bf16[8,96,512]{2,1,0:T(8,128)(2,1)S(1)} all-to-all(bf16[8,96,512]{2,1,0:T(8,128)(2,1)S(1)} %broadcast_in_dim.141), channel_id=1, replica_groups=mesh['segment'=2,'seq_0'=2,'seq_1'=4,'seq_2'=2,'head'=4] {'seq_0','seq_1'}, dimensions={0} | all-to-all | bytes 1572864 | tf_op jit(solution)/shard_map/all_to_all | solution.py:21
  505.4 44.9 %all-gather.6.cloned.1.call-done = bf16[768,1536]{1,0:T(8,128)(2,1)} async-done(((bf16[48,1536]{1,0:T(8,128)(2,1)}), bf16[768,1536]{1,0:T(8,128)(2,1)}) %all-gather.6.cloned.1.call-update) | async-done | bytes 2359312 | tf_op jit(solution)/shard_map/all_gather | solution.py:77
  562.6 18.7 %all_to_all.221 = bf16[4,128,1024]{2,1,0:T(8,128)(2,1)S(1)} all-to-all(bf16[4,128,1024]{2,1,0:T(8,128)(2,1)S(1)} %bitcast.672), channel_id=1, replica_groups=mesh['segment'=2,'seq_0'=2,'seq_1'=4,'seq_2'=2,'head'=4] {'head'}, dimensions={0} | all-to-all | bytes 2097152 | tf_op jit(solution)/shard_map/all_to_all | solution.py:54
  594.6 12.1 %all-to-all-done.26 = bf16[4,128,1024]{2,1,0:T(8,128)(2,1)} async-done(((bf16[4,128,1024]{2,1,0:T(8,128)(2,1)}), bf16[4,128,1024]{2,1,0:T(8,128)(2,1)}, u32[]{:S(2)}, u32[]{:S(2)}) %all-to-all-start.26) | async-done | bytes 1048608 | tf_op jit(solution)/shard_map/all_to_all | solution.py:21
  645.8 22.6 %all_to_all.223 = bf16[8,1536,48]{1,2,0:T(8,128)(2,1)S(1)} all-to-all(bf16[8,1536,48]{1,2,0:T(8,128)(2,1)} %reduce_sum.602), channel_id=1, replica_groups=mesh['segment'=2,'seq_0'=2,'seq_1'=4,'seq_2'=2,'head'=4] {'seq_0','seq_1'}, dimensions={0} | all-to-all | bytes 2359296 | tf_op jit(solution)/shard_map/all_to_all | solution.py:62
  695.6 17.3 %all_to_all.226 = bf16[8,96,512]{2,1,0:T(8,128)(2,1)} all-to-all(bf16[8,96,512]{2,1,0:T(8,128)(2,1)} %reduce_sum.608), channel_id=1, replica_groups=mesh['segment'=2,'seq_0'=2,'seq_1'=4,'seq_2'=2,'head'=4] {'seq_0','seq_1'}, dimensions={0} | all-to-all | bytes 1572864 | tf_op jit(solution)/shard_map/all_to_all | solution.py:62
  714.2 16.8 %all_to_all.227 = bf16[8,96,512]{2,1,0:T(8,128)(2,1)S(1)} all-to-all(bf16[8,96,512]{2,1,0:T(8,128)(2,1)S(1)} %broadcast_in_dim.145), channel_id=1, replica_groups=mesh['segment'=2,'seq_0'=2,'seq_1'=4,'seq_2'=2,'head'=4] {'seq_0','seq_1'}, dimensions={0} | all-to-all | bytes 1572864 | tf_op jit(solution)/shard_map/all_to_all | solution.py:21
  757.3 17.3 %all_to_all.230 = bf16[8,96,512]{2,1,0:T(8,128)(2,1)} all-to-all(bf16[8,96,512]{2,1,0:T(8,128)(2,1)} %reduce_sum.610), channel_id=1, replica_groups=mesh['segment'=2,'seq_0'=2,'seq_1'=4,'seq_2'=2,'head'=4] {'seq_0','seq_1'}, dimensions={0} | all-to-all | bytes 1572864 | tf_op jit(solution)/shard_map/all_to_all | solution.py:62
  776.0 16.8 %all_to_all.231 = bf16[8,96,512]{2,1,0:T(8,128)(2,1)S(1)} all-to-all(bf16[8,96,512]{2,1,0:T(8,128)(2,1)S(1)} %broadcast_in_dim.147), channel_id=1, replica_groups=mesh['segment'=2,'seq_0'=2,'seq_1'=4,'seq_2'=2,'head'=4] {'seq_0','seq_1'}, dimensions={0} | all-to-all | bytes 1572864 | tf_op jit(solution)/shard_map/all_to_all | solution.py:21
  808.2 44.9 %all-gather.8.cloned.1.call-done = bf16[768,1536]{1,0:T(8,128)(2,1)} async-done(((bf16[48,1536]{1,0:T(8,128)(2,1)}), bf16[768,1536]{1,0:T(8,128)(2,1)}) %all-gather.8.cloned.1.call-update) | async-done | bytes 2359312 | tf_op jit(solution)/shard_map/all_gather | solution.py:77
  872.2 14.5 %all-to-all-done.38 = bf16[4,128,1024]{2,1,0:T(8,128)(2,1)S(1)} async-done(((bf16[4,128,1024]{2,1,0:T(8,128)(2,1)}), bf16[4,128,1024]{2,1,0:T(8,128)(2,1)S(1)}, u32[]{:S(2)}, u32[]{:S(2)}) %all-to-all-start.38) | async-done | bytes 1048608 | tf_op jit(solution)/shard_map/all_to_all | solution.py:54
  (415 shorter events, 375.9 us)
Async XLA Ops:
  8.7 25.1 %all-to-all-start = ((bf16[4,128,1024]{2,1,0:T(8,128)(2,1)}), bf16[4,128,1024]{2,1,0:T(8,128)(2,1)S(1)}, u32[]{:S(2)}, u32[]{:S(2)}) async-start(bf16[4,128,1024]{2,1,0:T(8,128)(2,1)} %broadcast_in_dim.131), calls=%async_computation | async-start | bytes 2097152 | tf_op jit(solution)/shard_map/all_to_all | solution.py:21
  14.6 232.9 %all-gather.4.cloned.1.call-start = ((), (), s32[]{:S(2)}) async-start(), calls=%async_computation.39 | async-start | bytes 2506752 | tf_op jit(solution)/shard_map/all_gather | solution.py:77
  249.7 70.5 %copy-start.67 = (f32[512]{0:T(512)}, f32[512]{0:T(512)S(1)}, u32[]{:S(2)}) copy-start(f32[512]{0:T(512)S(1)} %add_divide_fusion.11) | copy-start | bytes 6148
  252.1 65.8 %copy-start.58 = (f32[768]{0:T(1024)}, f32[768]{0:T(1024)S(1)}, u32[]{:S(2)}) copy-start(f32[768]{0:T(1024)S(1)} %add_divide_fusion.8) | copy-start | bytes 9220
  252.1 66.4 %copy-start.55 = (f32[768]{0:T(1024)}, f32[768]{0:T(1024)S(1)}, u32[]{:S(2)}) copy-start(f32[768]{0:T(1024)S(1)} %add_divide_fusion.7) | copy-start | bytes 9220
  278.0 6.4 collective-permute-start
  286.3 16.8 %all-to-all-start.13 = ((bf16[4,128,1024]{2,1,0:T(8,128)(2,1)}), bf16[4,128,1024]{2,1,0:T(8,128)(2,1)}, u32[]{:S(2)}, u32[]{:S(2)}) async-start(bf16[4,128,1024]{2,1,0:T(8,128)(2,1)} %broadcast_in_dim.137), calls=%async_computation.13 | async-start | bytes 2097152 | tf_op jit(solution)/shard_map/all_to_all | solution.py:21
  290.5 259.8 %all-gather.6.cloned.1.call-start = ((), (), s32[]{:S(2)}) async-start(), calls=%async_computation.40 | async-start | bytes 2506752 | tf_op jit(solution)/shard_map/all_gather | solution.py:77
  502.6 47.8 %copy-start.68 = (f32[512]{0:T(512)S(1)}, f32[512]{0:T(512)}, u32[]{:S(2)}) copy-start(f32[512]{0:T(512)} %copy-done.67) | copy-start | bytes 6148
  504.7 47.4 %copy-start.62 = (f32[512]{0:T(512)S(1)}, f32[512]{0:T(512)}, u32[]{:S(2)}) copy-start(f32[512]{0:T(512)} %copy-done.61) | copy-start | bytes 6148
  504.7 47.4 %copy-start.56 = (f32[768]{0:T(1024)S(1)}, f32[768]{0:T(1024)}, u32[]{:S(2)}) copy-start(f32[768]{0:T(1024)} %copy-done.55) | copy-start | bytes 9220
  504.7 47.4 %copy-start.59 = (f32[768]{0:T(1024)S(1)}, f32[768]{0:T(1024)}, u32[]{:S(2)}) copy-start(f32[768]{0:T(1024)} %copy-done.58) | copy-start | bytes 9220
  552.2 71.2 %copy-start.75 = (f32[512]{0:T(512)}, f32[512]{0:T(512)S(1)}, u32[]{:S(2)}) copy-start(f32[512]{0:T(512)S(1)} %add_divide_fusion.10) | copy-start | bytes 6148
  555.2 65.7 %copy-start.73 = (f32[768]{0:T(1024)}, f32[768]{0:T(1024)S(1)}, u32[]{:S(2)}) copy-start(f32[768]{0:T(1024)S(1)} %add_divide_fusion.6) | copy-start | bytes 9220
  555.3 66.5 %copy-start.71 = (f32[768]{0:T(1024)}, f32[768]{0:T(1024)S(1)}, u32[]{:S(2)}) copy-start(f32[768]{0:T(1024)S(1)} %add_divide_fusion.5) | copy-start | bytes 9220
  581.6 6.4 collective-permute-start.1
  589.8 16.8 %all-to-all-start.26 = ((bf16[4,128,1024]{2,1,0:T(8,128)(2,1)}), bf16[4,128,1024]{2,1,0:T(8,128)(2,1)}, u32[]{:S(2)}, u32[]{:S(2)}) async-start(bf16[4,128,1024]{2,1,0:T(8,128)(2,1)} %broadcast_in_dim.143), calls=%async_computation.26 | async-start | bytes 2097152 | tf_op jit(solution)/shard_map/all_to_all | solution.py:21
  594.1 259.0 %all-gather.8.cloned.1.call-start = ((), (), s32[]{:S(2)}) async-start(), calls=%async_computation.41 | async-start | bytes 2506752 | tf_op jit(solution)/shard_map/all_gather | solution.py:77
  805.4 47.7 %copy-start.69 = (f32[512]{0:T(512)S(1)}, f32[512]{0:T(512)}, u32[]{:S(2)}) copy-start(f32[512]{0:T(512)} %copy-done.67) | copy-start | bytes 6148
  805.4 47.7 %copy-start.76 = (f32[512]{0:T(512)S(1)}, f32[512]{0:T(512)}, u32[]{:S(2)}) copy-start(f32[512]{0:T(512)} %copy-done.75) | copy-start | bytes 6148
  808.2 47.1 %copy-start.57 = (f32[768]{0:T(1024)S(1)}, f32[768]{0:T(1024)}, u32[]{:S(2)}) copy-start(f32[768]{0:T(1024)} %copy-done.55) | copy-start | bytes 9220
  808.2 47.1 %copy-start.60 = (f32[768]{0:T(1024)S(1)}, f32[768]{0:T(1024)}, u32[]{:S(2)}) copy-start(f32[768]{0:T(1024)} %copy-done.58) | copy-start | bytes 9220
  808.2 47.1 %copy-start.72 = (f32[768]{0:T(1024)S(1)}, f32[768]{0:T(1024)}, u32[]{:S(2)}) copy-start(f32[768]{0:T(1024)} %copy-done.71) | copy-start | bytes 9220
  867.8 18.9 %all-to-all-start.38 = ((bf16[4,128,1024]{2,1,0:T(8,128)(2,1)}), bf16[4,128,1024]{2,1,0:T(8,128)(2,1)S(1)}, u32[]{:S(2)}, u32[]{:S(2)}) async-start(bf16[4,128,1024]{2,1,0:T(8,128)(2,1)} %bitcast.643), calls=%async_computation.38 | async-start | bytes 2097152 | tf_op jit(solution)/shard_map/all_to_all | solution.py:54
  (71 other events, 408.5 us)
Sparse Core Ops, SparseCore 0:
  201.3 46.0 all-gather.3
  505.5 44.7 all-gather.5
  808.3 44.7 all-gather.7
where the time goes:
time: 906 us; the launch traced here: 895 us
  blocking collectives  445 us (49%)
  waiting for transfers between devices  181 us (20%)
  matrix products  93.7 us (10%)
  other arithmetic  68.2 us (8%)
  local copies, waits for them, and re-layouts  61.9 us (7%)
  starting transfers between devices  23.9 us (3%)
  between operations  21.3 us (2%)
    all_to_all x15, blocking collectives, from_everyone(): return lax.all_to_all(copies, axis, split_axis=0, concat_axis=0, tiled=True)  178 us
    all_to_all x9, blocking collectives, sum_by_axis(): lax.all_to_all(own.astype(jnp.bfloat16), far, 0, 0, tiled=True)  170 us
    all_gather x3, waiting for transfers between devices, gather_turned(): whole = lax.all_gather(both, axis, axis=0, tiled=True)  134 us
    all_to_all x11, blocking collectives, summed_on_arrival(): lax.all_to_all(in_blocks(array, dim, devices), axis, 0, 0, tiled=True)  97.4 us
    dot_general x18, matrix products, orthogonal_updates(): jnp.dot(mixing, block, preferred_element_type=jnp.float32)  30.6 us
    dot_general x3, matrix products, run_section(): projected = jnp.dot(normed, qkv_matrix, preferred_element_type=jnp.float32)  27.1 us
    unnamed x176, local copies, waits for them, and re-layouts  25.6 us
    all_to_all x3, waiting for transfers between devices, from_everyone(): return lax.all_to_all(copies, axis, split_axis=0, concat_axis=0, tiled=True)  24.7 us
  transfers between devices with their start and end apart: 9, of which 8 were waited for; matrix products, arithmetic and copies ran while one was open for 2% of the time, Pallas kernels for 0%

commit v1 on v0

v1 whole, which is shorter than its diff:
```python
import jax
import jax.numpy as jnp
from jax import lax
from jax.sharding import Mesh
from jax.sharding import PartitionSpec as P

NS_STEPS = 2
SEQ = ("seq_0", "seq_1", "seq_2")

ns_first = 3.4445
ns_second = -4.775
ns_third = 2.0315
norm_eps = 1e-06
grad_eps = 1e-07


def turned(array, axis, by):
    devices = lax.axis_size(axis)
    return lax.ppermute(array, axis, [(i, (i + by) % devices) for i in range(devices)])


def others(array, axis):
    return [turned(array, axis, by) for by in range(1, lax.axis_size(axis))]


def gathered_columns(array, axis):
    devices = lax.axis_size(axis)
    here = lax.axis_index(axis)
    rows, width = array.shape
    whole = jnp.zeros((rows, devices, width), array.dtype)
    whole = lax.dynamic_update_index_in_dim(whole, array, here, 1)
    for by in range(1, devices):
        piece = turned(array, axis, by)
        whole = lax.dynamic_update_index_in_dim(whole, piece, (here - by) % devices, 1)
    return whole.reshape(rows, devices * width)


def summed_columns(array, axis):
    devices = lax.axis_size(axis)
    here = lax.axis_index(axis)
    rows, width = array.shape
    pieces = array.reshape(rows, devices, width // devices)
    own = lax.dynamic_index_in_dim(pieces, here, 1, keepdims=False)
    total = own
    for by in range(1, devices):
        piece = lax.dynamic_index_in_dim(pieces, (here + by) % devices, 1, keepdims=False)
        total = total + turned(piece.astype(jnp.bfloat16), axis, by).astype(jnp.float32)
    return total


def all_tokens(block):
    across = turned(block, "seq_0", 1)
    blocks = [block, *others(block, "seq_1"), across, *others(across, "seq_1")]
    mine = jnp.concatenate(blocks, axis=0)
    return jnp.concatenate([mine, turned(mine, "seq_2", 1)], axis=0)


def rms_scale(values):
    return values * lax.rsqrt(jnp.mean(values * values, axis=-1, keepdims=True) + norm_eps)


def contract_rows(left, right):
    return lax.dot_general(
        left, right, (((0,), (0,)), ((), ())), preferred_element_type=jnp.float32
    )


def contract_columns(left, right):
    return lax.dot_general(
        left, right, (((1,), (1,)), ((), ())), preferred_element_type=jnp.float32
    )


def orthogonal(gradient):
    current = (gradient / (jnp.sqrt(jnp.sum(gradient * gradient)) + grad_eps)).astype(jnp.bfloat16)
    for _ in range(NS_STEPS):
        gram = contract_columns(current, current).astype(jnp.bfloat16)
        square = jnp.dot(gram, gram, preferred_element_type=jnp.float32)
        mixing = (ns_second * gram.astype(jnp.float32) + ns_third * square).astype(jnp.bfloat16)
        current = (
            ns_first * current.astype(jnp.float32)
            + jnp.dot(mixing, current, preferred_element_type=jnp.float32)
        ).astype(jnp.bfloat16)
    return current.astype(jnp.float32)


def renormalize(weights, target_norms, axis):
    sums = jnp.sum(weights * weights, axis=axis, keepdims=True)
    return weights * (target_norms / (jnp.sqrt(sums) + norm_eps))


def project(whole, gain_row, qkv_matrix, head_gains, rate_row):
    normed = (rms_scale(whole.astype(jnp.float32)) * gain_row).astype(jnp.bfloat16)
    projected = jnp.dot(normed, qkv_matrix, preferred_element_type=jnp.float32)
    projected = projected.reshape(whole.shape[0], 3, -1)
    queries = rms_scale(projected[:, 0]) * head_gains[0]
    key_rows = (rms_scale(projected[:, 1]) * head_gains[1]).astype(jnp.bfloat16)
    out_grad = (-rate_row[:, None] * projected[:, 2]).astype(jnp.bfloat16)
    return queries, jnp.concatenate([key_rows, out_grad], axis=1)


def trained(tokens, queries, fasts, norms, out_gain_row):
    width = tokens.shape[1] // 2
    key_rows, out_grad = tokens[:, :width], tokens[:, width:]
    gate_low, up_low, down_low = (f.astype(jnp.bfloat16) for f in fasts)
    pre_gate = jnp.dot(key_rows, gate_low, preferred_element_type=jnp.float32)
    pre_up = jnp.dot(key_rows, up_low, preferred_element_type=jnp.float32)
    sigmoid_gate = jax.nn.sigmoid(pre_gate)
    gated = pre_gate * sigmoid_gate
    hidden = (gated * pre_up).astype(jnp.bfloat16)
    backward = jnp.dot(out_grad, down_low, preferred_element_type=jnp.float32)
    grad_gate = (backward * pre_up * sigmoid_gate * (1.0 + pre_gate * (1.0 - sigmoid_gate))).astype(
        jnp.bfloat16
    )
    grad_up = (backward * gated).astype(jnp.bfloat16)
    shares = (
        contract_rows(key_rows, grad_gate),
        contract_rows(key_rows, grad_up),
        contract_rows(out_grad, hidden),
    )
    fresh = tuple(
        renormalize(fast - orthogonal(share), norm, axis)
        for fast, share, norm, axis in zip(fasts, shares, norms, (0, 0, 1))
    )
    gate_low, up_low, down_low = (f.astype(jnp.bfloat16) for f in fresh)
    queries = queries.astype(jnp.bfloat16)
    gate_out = jnp.dot(queries, gate_low, preferred_element_type=jnp.float32)
    up_out = jnp.dot(queries, up_low, preferred_element_type=jnp.float32)
    output = contract_columns((jax.nn.silu(gate_out) * up_out).astype(jnp.bfloat16), down_low)
    return (rms_scale(output) * out_gain_row).astype(jnp.bfloat16), fresh


def shards(stream, in_gain, w_qkv, qk_gain, w_one, w_three, w_two, token_rate, out_gain, w_out):
    segment_index = lax.axis_index("segment")
    span_count = stream.shape[0]
    qkv_matrix = w_qkv[0].reshape(w_qkv.shape[1], -1)
    initial = (
        w_one[0, 0].astype(jnp.float32),
        w_three[0, 0].astype(jnp.float32),
        w_two[0, 0].T.astype(jnp.float32),
    )
    norms = tuple(
        jnp.sqrt(jnp.sum(matrix * matrix, axis=axis, keepdims=True))
        for matrix, axis in zip(initial, (0, 0, 1))
    )

    def section(sources):
        prepared = []
        for span, source in enumerate(sources):
            queries, own = project(
                gathered_columns(source, "head"),
                in_gain[0],
                qkv_matrix,
                qk_gain[0, 0],
                token_rate[0, span],
            )
            prepared.append((queries, all_tokens(own)))
        fasts, results = initial, []
        for (queries, tokens), source in zip(prepared, sources):
            normed_out, fasts = trained(tokens, queries, fasts, norms, out_gain[0, 0])
            head_terms = jnp.dot(normed_out, w_out[0, 0], preferred_element_type=jnp.float32)
            delta = summed_columns(head_terms, "head")
            results.append((source.astype(jnp.float32) + delta).astype(jnp.bfloat16))
        return results

    results = section([stream[span] for span in range(span_count)])
    for _ in range(1, lax.axis_size("segment")):
        step = lax.axis_size("segment") - 1
        received = [lax.ppermute(r, "segment", [(i, i + 1) for i in range(step)]) for r in results]
        later = section(received)
        results = [
            jnp.where(segment_index == 0, r, fresh) for r, fresh in zip(results, later)
        ]
    return jnp.stack(results)[None]


def solution(mesh):
    torus = Mesh(
        mesh.devices.reshape(mesh.shape["segment"], 2, 4, 2, mesh.shape["head"]),
        ("segment", "seq_0", "seq_1", "seq_2", "head"),
    )
    return jax.shard_map(
        shards,
        mesh=torus,
        in_specs=(
            P(None, SEQ, "head"),
            P("segment", None),
            P("segment", None, "head", None, None),
            P("segment", "head", None, None),
            P("segment", "head", None, None),
            P("segment", "head", None, None),
            P("segment", "head", None, None),
            P("segment", None, SEQ),
            P("segment", "head", None),
            P("segment", "head", None, None),
        ),
        out_specs=P("segment", None, SEQ, "head"),
        check_vma=False,
    )
```

time: 906 us -> 659 us (0.73)
  blocking collectives: 445 us -> 0 us
  matrix products: 93.7 us -> 349 us
  waiting for transfers between devices: 181 us -> 95.3 us
  starting transfers between devices: 23.9 us -> 79.9 us
  other arithmetic: 68.2 us -> 22.8 us
  local copies, waits for them, and re-layouts: 61.9 us -> 96.2 us
  between operations: 21.3 us -> 9.52 us
    all_to_all x35 -> x0, blocking collectives: 445 us -> none  [the longest x15 178 us: from_everyone(): return lax.all_to_all(copies, axis, split_axis=0, concat_axis=0, tiled=True)]
    dot_general x60 -> x76, matrix products: 89.7 us -> 277 us  [the longest x24 97.6 us: orthogonal(): jnp.dot(mixing, current, preferred_element_type=jnp.float32)]
    all_gather x3 -> x0, waiting for transfers between devices: 134 us -> none  [gather_turned(): whole = lax.all_gather(both, axis, axis=0, tiled=True)]
    ppermute x2 -> x58, waiting for transfers between devices: 7.94 us -> 95.3 us  [the longest x56 90 us: turned(): lax.ppermute(array, axis, [(i, (i + by) % devices) for i in range(devices)])]
    ppermute x2 -> x58, starting transfers between devices: 4.81 us -> 79.9 us  [the longest x56 75.7 us: turned(): lax.ppermute(array, axis, [(i, (i + by) % devices) for i in range(devices)])]
    dot_general x9 -> x12, matrix products: 4.05 us -> 72.3 us  [contract_rows(): lax.dot_general(left, right, (((0,), (0,)), ((), ())), preferred_element_...]
    reduce_sum x33 -> x0, other arithmetic: 44.2 us -> none  [the longest x12 22 us: summed_on_arrival(): return jnp.sum(pieces.astype(jnp.float32), axis=0)]
    all_to_all x4 -> x0, waiting for transfers between devices: 39.2 us -> none  [the longest x3 24.7 us: from_everyone(): return lax.all_to_all(copies, axis, split_axis=0, concat_axis=0, tiled=True)]
  transfers between devices with their start and end apart: 9 -> 58, of which waited for: 8 -> 31; matrix products, arithmetic and copies ran while one was open for 2% -> 42% of each run, Pallas kernels for 0% -> 0%
where the time goes in v1:
time: 659 us; the launch traced here: 653 us
  matrix products  349 us (53%)
  local copies, waits for them, and re-layouts  96.2 us (15%)
  waiting for transfers between devices  95.3 us (14%)
  starting transfers between devices  79.9 us (12%)
  other arithmetic  22.8 us (3%)
  between operations  9.52 us (1%)
    dot_general x24, matrix products, orthogonal(): jnp.dot(mixing, current, preferred_element_type=jnp.float32)  97.6 us
    ppermute x56, waiting for transfers between devices, turned(): lax.ppermute(array, axis, [(i, (i + by) % devices) for i in range(devices)])  90 us
    dot_general x28, matrix products, contract_columns(): lax.dot_general(left, right, (((1,), (1,)), ((), ())), preferred_element_...  82.4 us
    ppermute x56, starting transfers between devices, turned(): lax.ppermute(array, axis, [(i, (i + by) % devices) for i in range(devices)])  75.7 us
    dot_general x12, matrix products, contract_rows(): lax.dot_general(left, right, (((0,), (0,)), ((), ())), preferred_element_...  72.3 us
    unnamed x153, local copies, waits for them, and re-layouts  42.9 us
    dot_general x4, matrix products, project(): projected = jnp.dot(normed, qkv_matrix, preferred_element_type=jnp.float32)  35.8 us
    dot_general x4, matrix products, section(): jnp.dot(normed_out, w_out[0, 0], preferred_element_type=jnp.float32)  15.2 us
  transfers between devices with their start and end apart: 58, of which 31 were waited for; matrix products, arithmetic and copies ran while one was open for 42% of the time, Pallas kernels for 0%

profile of v1, /device:TPU:1, one launch (start us, length us, event | category | flops | bytes accessed | tf_op | source)
XLA Modules:
  0.0 653.2 jit_solution(10414305393639082368)
XLA Ops:
  11.3 16.9 %copy.27 = bf16[1,4096,1,3,512]{1,4,3,2,0:T(8,128)(2,1)} copy(bf16[1,4096,1,3,512]{4,1,3,2,0:T(8,128)(2,1)} %param.12) | data formatting | bytes 25165824 | tf_op args[2]
  38.6 8.8 %fusion.6 = f32[128,3,512]{2,0,1:T(8,128)S(1)} fusion(bf16[128,4096,1]{1,0,2:T(8,128)(2,1)S(1)} %reshape.353, bf16[1,4096,1,3,512]{1,4,3,2,0:T(8,128)(2,1)} %copy.27), kind=kOutput, calls=%fused_computation.6 | convolution fusion | flops 1610612736 | bytes 14417920 | tf_op jit(solution)/shard_map/dot_general | solution.py:94
  50.4 8.8 %fusion.2 = f32[128,3,512]{2,0,1:T(8,128)S(1)} fusion(bf16[128,4096,1]{1,0,2:T(8,128)(2,1)S(1)} %reshape.357, bf16[1,4096,1,3,512]{1,4,3,2,0:T(8,128)(2,1)} %copy.27), kind=kOutput, calls=%fused_computation.2 | convolution fusion | flops 1610612736 | bytes 14417920 | tf_op jit(solution)/shard_map/dot_general | solution.py:94
  93.1 6.5 %copy.40 = bf16[4096,512]{1,0:T(8,128)(2,1)} copy(bf16[4096,512]{0,1:T(8,128)(2,1)} %bitcast.431) | data formatting | bytes 8388608 | tf_op jit(solution)/shard_map/dot_general | solution.py:161
  105.7 7.1 %collective-permute-done.35 = bf16[128,1024]{1,0:T(8,128)(2,1)S(1)} collective-permute-done((bf16[128,1024]{1,0:T(8,128)(2,1)S(1)}, bf16[128,1024]{1,0:T(8,128)(2,1)S(1)}, u32[]{:S(2)}, u32[]{:S(2)}) %collective-permute-start.35) | collective-permute-done | bytes 262176 | tf_op jit(solution)/shard_map/ppermute | solution.py:19
  144.9 5.5 multiply_reduce_fusion.19
  150.4 6.6 %multiply_reduce_fusion.23 = (f32[]{:T(128)}, f32[512,768]{1,0:T(8,128)}) fusion(f32[2048,768]{1,0:T(8,128)S(1)} %fusion.104, f32[2048,768]{1,0:T(8,128)S(1)} %fusion.43, f32[2048,768]{1,0:T(8,128)S(1)} %fusion.106, bf16[2048,1024]{1,0:T(8,128)(2,1)} %constant_dynamic-update-slice_fusion.8), kind=kOutput, calls=%fused_computation.153 | convolution fusion | flops 1627127808 | bytes 22544388 | tf_op jit(solution)/shard_map/dot_general | solution.py:63
  157.0 5.6 multiply_reduce_fusion.21
  214.6 6.2 multiply_reduce_fusion.7
  224.2 5.6 multiply_reduce_fusion.9
  229.9 6.7 %multiply_reduce_fusion.11 = (f32[]{:T(128)}, f32[512,768]{1,0:T(8,128)}) fusion(f32[2048,768]{1,0:T(8,128)S(1)} %fusion.92, f32[2048,768]{1,0:T(8,128)S(1)} %fusion.37, f32[2048,768]{1,0:T(8,128)S(1)} %fusion.94, bf16[2048,1024]{1,0:T(8,128)(2,1)} %constant_dynamic-update-slice_fusion.42), kind=kOutput, calls=%fused_computation.123 | convolution fusion | flops 1627127808 | bytes 22544388 | tf_op jit(solution)/shard_map/dot_general | solution.py:63
  315.0 7.1 %collective-permute-done.40 = bf16[128,1024]{1,0:T(8,128)(2,1)S(1)} collective-permute-done((bf16[128,1024]{1,0:T(8,128)(2,1)S(1)}, bf16[128,1024]{1,0:T(8,128)(2,1)S(1)}, u32[]{:S(2)}, u32[]{:S(2)}) %collective-permute-start.40) | collective-permute-done | bytes 262176 | tf_op jit(solution)/shard_map/ppermute | solution.py:19
  341.7 5.5 collective-permute-done.17
  351.7 8.9 %fusion.4 = f32[128,3,512]{2,0,1:T(8,128)S(1)} fusion(bf16[128,4096,1]{1,0,2:T(8,128)(2,1)S(1)} %reshape.355, bf16[1,4096,1,3,512]{1,4,3,2,0:T(8,128)(2,1)} %copy.27), kind=kOutput, calls=%fused_computation.4 | convolution fusion | flops 1610612736 | bytes 14417920 | tf_op jit(solution)/shard_map/dot_general | solution.py:94
  365.9 7.9 %dynamic_update_slice.64 = bf16[128,4,1024]{2,1,0:T(4,128)(2,1)S(1)} dynamic-update-slice(bf16[128,4,1024]{2,1,0:T(4,128)(2,1)S(1)} %copy.35, bf16[128,1,1024]{2,1,0:T(2,128)(2,1)} %copy.36, s32[]{:T(128)} %constant.183.clone.1, s32[]{:T(128)S(6)} %select_n.130, s32[]{:T(128)} %constant.183.clone.1) | dynamic-update-slice | bytes 524292 | tf_op jit(solution)/shard_map/jit(dynamic_update_index_in_dim)/dynamic_update_slice | solution.py:34
  379.9 9.2 %fusion = f32[128,3,512]{2,0,1:T(8,128)S(1)} fusion(bf16[128,4096,1]{1,0,2:T(8,128)(2,1)} %reshape.359, bf16[1,4096,1,3,512]{1,4,3,2,0:T(8,128)(2,1)} %copy.27), kind=kOutput, calls=%fused_computation | convolution fusion | flops 1610612736 | bytes 14417920 | tf_op jit(solution)/shard_map/dot_general | solution.py:94
  427.5 6.5 collective-permute-done.50
  466.1 5.6 multiply_reduce_fusion.15
  471.6 6.5 %multiply_reduce_fusion.17 = (f32[]{:T(128)}, f32[512,768]{1,0:T(8,128)}) fusion(f32[2048,768]{1,0:T(8,128)S(1)} %fusion.98, f32[2048,768]{1,0:T(8,128)S(1)} %fusion.40, f32[2048,768]{1,0:T(8,128)S(1)} %fusion.100, bf16[2048,1024]{1,0:T(8,128)(2,1)} %constant_dynamic-update-slice_fusion.25), kind=kOutput, calls=%fused_computation.138 | convolution fusion | flops 1627127808 | bytes 22544388 | tf_op jit(solution)/shard_map/dot_general | solution.py:63
  478.2 5.8 multiply_reduce_fusion.13
  539.3 6.1 multiply_reduce_fusion.1
  548.9 5.6 multiply_reduce_fusion.3
  554.5 6.6 %multiply_reduce_fusion.5 = (f32[]{:T(128)}, f32[512,768]{1,0:T(8,128)}) fusion(f32[2048,768]{1,0:T(8,128)S(1)} %fusion.86, f32[2048,768]{1,0:T(8,128)S(1)} %fusion.34, f32[2048,768]{1,0:T(8,128)S(1)} %fusion.88, bf16[2048,1024]{1,0:T(8,128)(2,1)} %constant_dynamic-update-slice_fusion.59), kind=kOutput, calls=%fused_computation.102 | convolution fusion | flops 1627127808 | bytes 22544388 | tf_op jit(solution)/shard_map/dot_general | solution.py:63
  642.0 6.1 collective-permute-done.28
  (430 shorter events, 471.9 us)
Async XLA Ops:
  1.9 26.3 %collective-permute-start.29 = (bf16[128,1024]{1,0:T(8,128)(2,1)}, bf16[128,1024]{1,0:T(8,128)(2,1)}, u32[]{:S(2)}, u32[]{:S(2)}) collective-permute-start(bf16[128,1024]{1,0:T(8,128)(2,1)} %get-tuple-element.42), channel_id=1, source_target_pairs={{0,1},{1,2},{2,3},{3,0},{4,5},{5,6},{6,7},{7,4},{8,9},{9,10},{10,1... | collective-permute-start | bytes 786440 | tf_op jit(solution)/shard_map/ppermute | solution.py:19
  4.4 28.1 %collective-permute-start.30 = (bf16[128,1024]{1,0:T(8,128)(2,1)}, bf16[128,1024]{1,0:T(8,128)(2,1)S(1)}, u32[]{:S(2)}, u32[]{:S(2)}) collective-permute-start(bf16[128,1024]{1,0:T(8,128)(2,1)} %get-tuple-element.42), channel_id=1, source_target_pairs={{0,2},{1,3},{2,0},{3,1},{4,6},{5,7},{6,4},{7,5},{8,10},{9,11},{10,... | collective-permute-start | bytes 786440 | tf_op jit(solution)/shard_map/ppermute | solution.py:19
  7.7 24.8 %collective-permute-start.31 = (bf16[128,1024]{1,0:T(8,128)(2,1)}, bf16[128,1024]{1,0:T(8,128)(2,1)}, u32[]{:S(2)}, u32[]{:S(2)}) collective-permute-start(bf16[128,1024]{1,0:T(8,128)(2,1)} %get-tuple-element.42), channel_id=1, source_target_pairs={{0,3},{1,0},{2,1},{3,2},{4,7},{5,4},{6,5},{7,6},{8,11},{9,8},{10,9... | collective-permute-start | bytes 786440 | tf_op jit(solution)/shard_map/ppermute | solution.py:19
  8.4 23.0 %collective-permute-start = (bf16[128,1024]{1,0:T(8,128)(2,1)}, bf16[128,1024]{1,0:T(8,128)(2,1)}, u32[]{:S(2)}, u32[]{:S(2)}) collective-permute-start(bf16[128,1024]{1,0:T(8,128)(2,1)} %get-tuple-element.41), channel_id=1, source_target_pairs={{0,1},{1,2},{2,3},{3,0},{4,5},{5,6},{6,7},{7,4},{8,9},{9,10},{10,1... | collective-permute-start | bytes 786440 | tf_op jit(solution)/shard_map/ppermute | solution.py:19
  9.2 23.3 %collective-permute-start.1 = (bf16[128,1024]{1,0:T(8,128)(2,1)}, bf16[128,1024]{1,0:T(8,128)(2,1)S(1)}, u32[]{:S(2)}, u32[]{:S(2)}) collective-permute-start(bf16[128,1024]{1,0:T(8,128)(2,1)} %get-tuple-element.41), channel_id=1, source_target_pairs={{0,2},{1,3},{2,0},{3,1},{4,6},{5,7},{6,4},{7,5},{8,10},{9,11},{10,... | collective-permute-start | bytes 786440 | tf_op jit(solution)/shard_map/ppermute | solution.py:19
  68.2 15.7 %collective-permute-start.7 = (bf16[128,1024]{1,0:T(8,128)(2,1)S(1)}, bf16[128,1024]{1,0:T(8,128)(2,1)S(1)}, u32[]{:S(2)}, u32[]{:S(2)}) collective-permute-start(bf16[128,1024]{1,0:T(8,128)(2,1)S(1)} %collective-permute-done.6), channel_id=1, source_target_pairs={{0,8},{8,16},{16,24},{24,0},{1,9},{9,17},{17,25},{25,1},{2,10},{10... | collective-permute-start | bytes 786440 | tf_op jit(solution)/shard_map/ppermute | solution.py:19
  69.1 18.0 %collective-permute-start.8 = (bf16[128,1024]{1,0:T(8,128)(2,1)S(1)}, bf16[128,1024]{1,0:T(8,128)(2,1)S(1)}, u32[]{:S(2)}, u32[]{:S(2)}) collective-permute-start(bf16[128,1024]{1,0:T(8,128)(2,1)S(1)} %collective-permute-done.6), channel_id=1, source_target_pairs={{0,16},{8,24},{16,0},{24,8},{1,17},{9,25},{17,1},{25,9},{2,18},{10... | collective-permute-start | bytes 786440 | tf_op jit(solution)/shard_map/ppermute | solution.py:19
  71.7 16.3 %collective-permute-start.9 = (bf16[128,1024]{1,0:T(8,128)(2,1)S(1)}, bf16[128,1024]{1,0:T(8,128)(2,1)S(1)}, u32[]{:S(2)}, u32[]{:S(2)}) collective-permute-start(bf16[128,1024]{1,0:T(8,128)(2,1)S(1)} %collective-permute-done.6), channel_id=1, source_target_pairs={{0,24},{8,0},{16,8},{24,16},{1,25},{9,1},{17,9},{25,17},{2,26},{10... | collective-permute-start | bytes 786440 | tf_op jit(solution)/shard_map/ppermute | solution.py:19
  88.9 42.3 %collective-permute-start.10 = (bf16[1024,1024]{1,0:T(8,128)(2,1)}, bf16[1024,1024]{1,0:T(8,128)(2,1)}, u32[]{:S(2)}, u32[]{:S(2)}) collective-permute-start(bf16[1024,1024]{1,0:T(8,128)(2,1)} %get-tuple-element.77), channel_id=1, source_target_pairs={{0,4},{4,0},{1,5},{5,1},{2,6},{6,2},{3,7},{7,3},{8,12},{12,8},{9,1... | collective-permute-start | bytes 6291464 | tf_op jit(solution)/shard_map/ppermute | solution.py:19
  100.8 15.6 %collective-permute-start.33 = (bf16[128,1024]{1,0:T(8,128)(2,1)S(1)}, bf16[128,1024]{1,0:T(8,128)(2,1)S(1)}, u32[]{:S(2)}, u32[]{:S(2)}) collective-permute-start(bf16[128,1024]{1,0:T(8,128)(2,1)S(1)} %get-tuple-element.110), channel_id=1, source_target_pairs={{0,16},{8,24},{16,0},{24,8},{1,17},{9,25},{17,1},{25,9},{2,18},{10... | collective-permute-start | bytes 786440 | tf_op jit(solution)/shard_map/ppermute | solution.py:19
  127.7 76.6 %collective-permute-start.39 = (bf16[1024,1024]{1,0:T(8,128)(2,1)}, bf16[1024,1024]{1,0:T(8,128)(2,1)}, u32[]{:S(2)}, u32[]{:S(2)}) collective-permute-start(bf16[1024,1024]{1,0:T(8,128)(2,1)} %get-tuple-element.94), channel_id=1, source_target_pairs={{0,4},{4,0},{1,5},{5,1},{2,6},{6,2},{3,7},{7,3},{8,12},{12,8},{9,1... | collective-permute-start | bytes 6291464 | tf_op jit(solution)/shard_map/ppermute | solution.py:19
  247.2 60.9 %collective-permute-start.13 = (bf16[128,1024]{1,0:T(8,128)(2,1)}, bf16[128,1024]{1,0:T(8,128)(2,1)}, u32[]{:S(2)}, u32[]{:S(2)}) collective-permute-start(bf16[128,1024]{1,0:T(8,128)(2,1)} %get-tuple-element.26), channel_id=1, source_target_pairs={{0,3},{1,0},{2,1},{3,2},{4,7},{5,4},{6,5},{7,6},{8,11},{9,8},{10,9... | collective-permute-start | bytes 786440 | tf_op jit(solution)/shard_map/ppermute | solution.py:19
  249.7 58.4 %collective-permute-start.12 = (bf16[128,1024]{1,0:T(8,128)(2,1)}, bf16[128,1024]{1,0:T(8,128)(2,1)}, u32[]{:S(2)}, u32[]{:S(2)}) collective-permute-start(bf16[128,1024]{1,0:T(8,128)(2,1)} %get-tuple-element.27), channel_id=1, source_target_pairs={{0,2},{1,3},{2,0},{3,1},{4,6},{5,7},{6,4},{7,5},{8,10},{9,11},{10,... | collective-permute-start | bytes 786440 | tf_op jit(solution)/shard_map/ppermute | solution.py:19
  250.2 57.9 %collective-permute-start.11 = (bf16[128,1024]{1,0:T(8,128)(2,1)}, bf16[128,1024]{1,0:T(8,128)(2,1)}, u32[]{:S(2)}, u32[]{:S(2)}) collective-permute-start(bf16[128,1024]{1,0:T(8,128)(2,1)} %get-tuple-element.25), channel_id=1, source_target_pairs={{0,1},{1,2},{2,3},{3,0},{4,5},{5,6},{6,7},{7,4},{8,9},{9,10},{10,1... | collective-permute-start | bytes 786440 | tf_op jit(solution)/shard_map/ppermute | solution.py:19
  336.9 23.8 %collective-permute-start.44 = (bf16[128,1024]{1,0:T(8,128)(2,1)}, bf16[128,1024]{1,0:T(8,128)(2,1)}, u32[]{:S(2)}, u32[]{:S(2)}) collective-permute-start(bf16[128,1024]{1,0:T(8,128)(2,1)} %collective-permute-done.43), channel_id=1, source_target_pairs={{0,1},{1,2},{2,3},{3,0},{4,5},{5,6},{6,7},{7,4},{8,9},{9,10},{10,1... | collective-permute-start | bytes 786440 | tf_op jit(solution)/shard_map/ppermute | solution.py:19
  336.9 25.0 %collective-permute-start.45 = (bf16[128,1024]{1,0:T(8,128)(2,1)}, bf16[128,1024]{1,0:T(8,128)(2,1)}, u32[]{:S(2)}, u32[]{:S(2)}) collective-permute-start(bf16[128,1024]{1,0:T(8,128)(2,1)} %collective-permute-done.43), channel_id=1, source_target_pairs={{0,2},{1,3},{2,0},{3,1},{4,6},{5,7},{6,4},{7,5},{8,10},{9,11},{10,... | collective-permute-start | bytes 786440 | tf_op jit(solution)/shard_map/ppermute | solution.py:19
  341.2 22.6 %collective-permute-start.46 = (bf16[128,1024]{1,0:T(8,128)(2,1)}, bf16[128,1024]{1,0:T(8,128)(2,1)}, u32[]{:S(2)}, u32[]{:S(2)}) collective-permute-start(bf16[128,1024]{1,0:T(8,128)(2,1)} %collective-permute-done.43), channel_id=1, source_target_pairs={{0,3},{1,0},{2,1},{3,2},{4,7},{5,4},{6,5},{7,6},{8,11},{9,8},{10,9... | collective-permute-start | bytes 786440 | tf_op jit(solution)/shard_map/ppermute | solution.py:19
  397.1 15.6 %collective-permute-start.22 = (bf16[128,1024]{1,0:T(8,128)(2,1)S(1)}, bf16[128,1024]{1,0:T(8,128)(2,1)S(1)}, u32[]{:S(2)}, u32[]{:S(2)}) collective-permute-start(bf16[128,1024]{1,0:T(8,128)(2,1)S(1)} %collective-permute-done.21), channel_id=1, source_target_pairs={{0,8},{8,16},{16,24},{24,0},{1,9},{9,17},{17,25},{25,1},{2,10},{10... | collective-permute-start | bytes 786440 | tf_op jit(solution)/shard_map/ppermute | solution.py:19
  397.5 16.5 %collective-permute-start.23 = (bf16[128,1024]{1,0:T(8,128)(2,1)S(1)}, bf16[128,1024]{1,0:T(8,128)(2,1)S(1)}, u32[]{:S(2)}, u32[]{:S(2)}) collective-permute-start(bf16[128,1024]{1,0:T(8,128)(2,1)S(1)} %collective-permute-done.21), channel_id=1, source_target_pairs={{0,16},{8,24},{16,0},{24,8},{1,17},{9,25},{17,1},{25,9},{2,18},{10... | collective-permute-start | bytes 786440 | tf_op jit(solution)/shard_map/ppermute | solution.py:19
  400.5 15.6 %collective-permute-start.24 = (bf16[128,1024]{1,0:T(8,128)(2,1)S(1)}, bf16[128,1024]{1,0:T(8,128)(2,1)S(1)}, u32[]{:S(2)}, u32[]{:S(2)}) collective-permute-start(bf16[128,1024]{1,0:T(8,128)(2,1)S(1)} %collective-permute-done.21), channel_id=1, source_target_pairs={{0,24},{8,0},{16,8},{24,16},{1,25},{9,1},{17,9},{25,17},{2,26},{10... | collective-permute-start | bytes 786440 | tf_op jit(solution)/shard_map/ppermute | solution.py:19
  417.0 35.5 %collective-permute-start.25 = (bf16[1024,1024]{1,0:T(8,128)(2,1)}, bf16[1024,1024]{1,0:T(8,128)(2,1)}, u32[]{:S(2)}, u32[]{:S(2)}) collective-permute-start(bf16[1024,1024]{1,0:T(8,128)(2,1)} %get-tuple-element.43), channel_id=1, source_target_pairs={{0,4},{4,0},{1,5},{5,1},{2,6},{6,2},{3,7},{7,3},{8,12},{12,8},{9,1... | collective-permute-start | bytes 6291464 | tf_op jit(solution)/shard_map/ppermute | solution.py:19
  422.5 15.7 %collective-permute-start.48 = (bf16[128,1024]{1,0:T(8,128)(2,1)S(1)}, bf16[128,1024]{1,0:T(8,128)(2,1)S(1)}, u32[]{:S(2)}, u32[]{:S(2)}) collective-permute-start(bf16[128,1024]{1,0:T(8,128)(2,1)S(1)} %get-tuple-element.76), channel_id=1, source_target_pairs={{0,16},{8,24},{16,0},{24,8},{1,17},{9,25},{17,1},{25,9},{2,18},{10... | collective-permute-start | bytes 786440 | tf_op jit(solution)/shard_map/ppermute | solution.py:19
  449.1 80.0 %collective-permute-start.54 = (bf16[1024,1024]{1,0:T(8,128)(2,1)}, bf16[1024,1024]{1,0:T(8,128)(2,1)}, u32[]{:S(2)}, u32[]{:S(2)}) collective-permute-start(bf16[1024,1024]{1,0:T(8,128)(2,1)} %get-tuple-element.60), channel_id=1, source_target_pairs={{0,4},{4,0},{1,5},{5,1},{2,6},{6,2},{3,7},{7,3},{8,12},{12,8},{9,1... | collective-permute-start | bytes 6291464 | tf_op jit(solution)/shard_map/ppermute | solution.py:19
  632.4 15.6 %collective-permute-start.28 = (bf16[128,1024]{1,0:T(8,128)(2,1)S(1)}, bf16[128,1024]{1,0:T(8,128)(2,1)S(1)}, u32[]{:S(2)}, u32[]{:S(2)}) collective-permute-start(bf16[128,1024]{1,0:T(8,128)(2,1)S(1)} %get-tuple-element.20), channel_id=1, source_target_pairs={{0,3},{1,0},{2,1},{3,2},{4,7},{5,4},{6,5},{7,6},{8,11},{9,8},{10,9... | collective-permute-start | bytes 786440 | tf_op jit(solution)/shard_map/ppermute | solution.py:19
  (97 other events, 1424.7 us)

commit v2 on v1

--- a/solution.py
+++ b/solution.py
@@ -1,6 +1,8 @@
 import jax
 import jax.numpy as jnp
 from jax import lax
+from jax.experimental import pallas as pl
+from jax.experimental.pallas import tpu as pltpu
 from jax.sharding import Mesh
 from jax.sharding import PartitionSpec as P
 
@@ -59,34 +61,14 @@
     return values * lax.rsqrt(jnp.mean(values * values, axis=-1, keepdims=True) + norm_eps)
 
 
-def contract_rows(left, right):
-    return lax.dot_general(
-        left, right, (((0,), (0,)), ((), ())), preferred_element_type=jnp.float32
-    )
-
-
 def contract_columns(left, right):
     return lax.dot_general(
         left, right, (((1,), (1,)), ((), ())), preferred_element_type=jnp.float32
     )
 
 
-def orthogonal(gradient):
-    current = (gradient / (jnp.sqrt(jnp.sum(gradient * gradient)) + grad_eps)).astype(jnp.bfloat16)
-    for _ in range(NS_STEPS):
-        gram = contract_columns(current, current).astype(jnp.bfloat16)
-        square = jnp.dot(gram, gram, preferred_element_type=jnp.float32)
-        mixing = (ns_second * gram.astype(jnp.float32) + ns_third * square).astype(jnp.bfloat16)
-        current = (
-            ns_first * current.astype(jnp.float32)
-            + jnp.dot(mixing, current, preferred_element_type=jnp.float32)
-        ).astype(jnp.bfloat16)
-    return current.astype(jnp.float32)
-
-
-def renormalize(weights, target_norms, axis):
-    sums = jnp.sum(weights * weights, axis=axis, keepdims=True)
-    return weights * (target_norms / (jnp.sqrt(sums) + norm_eps))
+def product(left, right):
+    return jnp.dot(left, right, preferred_element_type=jnp.float32)
 
 
 def project(whole, gain_row, qkv_matrix, head_gains, rate_row):
@@ -99,35 +81,124 @@
     return queries, jnp.concatenate([key_rows, out_grad], axis=1)
 
 
+def update_kernel(
+    tokens,
+    queries,
+    gate,
+    up,
+    down,
+    gate_norm,
+    up_norm,
+    down_norm,
+    out_gain,
+    normed_out,
+    gate_new,
+    up_new,
+    down_new,
+    lows,
+    turned_keys,
+    turned_grads,
+    grads,
+    shares,
+    iterate,
+):
+    count, width = tokens.shape[0], queries.shape[1]
+    inner = gate.shape[1]
+    rows, columns = 512, 256
+    lows[0] = gate[...].astype(jnp.bfloat16)
+    lows[1] = up[...].astype(jnp.bfloat16)
+    lows[2] = down[...].astype(jnp.bfloat16)
+
+    @pl.loop(0, count // rows)
+    def _(step):
+        lines = pl.ds(pl.multiple_of(step * rows, rows), rows)
+        key_rows = tokens[lines, :width]
+        out_grad = tokens[lines, width:]
+        turned_keys[:, lines] = key_rows.T
+        turned_grads[:, lines] = out_grad.T
+        for start in range(0, inner, columns):
+            part = slice(start, start + columns)
+            pre_gate = product(key_rows, lows[0, :, part])
+            pre_up = product(key_rows, lows[1, :, part])
+            backward = product(out_grad, lows[2, :, part])
+            sigmoid_gate = 0.5 + 0.5 * jnp.tanh(0.5 * pre_gate)
+            gated = pre_gate * sigmoid_gate
+            slope = sigmoid_gate + gated * (1.0 - sigmoid_gate)
+            grads[0, lines, part] = (backward * pre_up * slope).astype(jnp.bfloat16)
+            grads[1, lines, part] = (backward * gated).astype(jnp.bfloat16)
+            grads[2, lines, part] = (gated * pre_up).astype(jnp.bfloat16)
+
+    for index, left in enumerate((turned_keys, turned_keys, turned_grads)):
+        squares = jnp.zeros((1, columns), jnp.float32)
+        for start in range(0, inner, columns):
+            part = slice(start, start + columns)
+            share = product(left[...], grads[index, :, part])
+            squares = squares + jnp.sum(share * share, axis=0, keepdims=True)
+            shares[index, :, part] = share
+        total = jnp.sum(squares, axis=1, keepdims=True)
+        scale = 1.0 / (jnp.sqrt(total) + grad_eps)
+        iterate[index] = (shares[index] * scale).astype(jnp.bfloat16)
+
+    for _ in range(NS_STEPS):
+        for index in range(3):
+            block = iterate[index]
+            gram = contract_columns(block, block).astype(jnp.bfloat16)
+            square = product(gram, gram)
+            mixing = (ns_second * gram.astype(jnp.float32) + ns_third * square).astype(jnp.bfloat16)
+            moved = product(mixing, block)
+            iterate[index] = (ns_first * block.astype(jnp.float32) + moved).astype(jnp.bfloat16)
+
+    fresh = []
+    for index, (fast, norm, result, axis) in enumerate(
+        (
+            (gate, gate_norm, gate_new, 0),
+            (up, up_norm, up_new, 0),
+            (down, down_norm, down_new, 1),
+        )
+    ):
+        moved = fast[...] - iterate[index].astype(jnp.float32)
+        sums = jnp.sum(moved * moved, axis=axis, keepdims=True)
+        moved = moved * (norm[...] / (jnp.sqrt(sums) + norm_eps))
+        result[...] = moved
+        fresh.append(moved.astype(jnp.bfloat16))
+    gate_low, up_low, down_low = fresh
+    low_queries = queries[...].astype(jnp.bfloat16)
+    gate_out = product(low_queries, gate_low)
+    up_out = product(low_queries, up_low)
+    hidden = gate_out * (0.5 + 0.5 * jnp.tanh(0.5 * gate_out)) * up_out
+    output = contract_columns(hidden.astype(jnp.bfloat16), down_low)
+    normed_out[...] = (rms_scale(output) * out_gain[...]).astype(jnp.bfloat16)
+
+
 def trained(tokens, queries, fasts, norms, out_gain_row):
-    width = tokens.shape[1] // 2
-    key_rows, out_grad = tokens[:, :width], tokens[:, width:]
-    gate_low, up_low, down_low = (f.astype(jnp.bfloat16) for f in fasts)
-    pre_gate = jnp.dot(key_rows, gate_low, preferred_element_type=jnp.float32)
-    pre_up = jnp.dot(key_rows, up_low, preferred_element_type=jnp.float32)
-    sigmoid_gate = jax.nn.sigmoid(pre_gate)
-    gated = pre_gate * sigmoid_gate
-    hidden = (gated * pre_up).astype(jnp.bfloat16)
-    backward = jnp.dot(out_grad, down_low, preferred_element_type=jnp.float32)
-    grad_gate = (backward * pre_up * sigmoid_gate * (1.0 + pre_gate * (1.0 - sigmoid_gate))).astype(
-        jnp.bfloat16
-    )
-    grad_up = (backward * gated).astype(jnp.bfloat16)
-    shares = (
-        contract_rows(key_rows, grad_gate),
-        contract_rows(key_rows, grad_up),
-        contract_rows(out_grad, hidden),
-    )
-    fresh = tuple(
-        renormalize(fast - orthogonal(share), norm, axis)
-        for fast, share, norm, axis in zip(fasts, shares, norms, (0, 0, 1))
-    )
-    gate_low, up_low, down_low = (f.astype(jnp.bfloat16) for f in fresh)
-    queries = queries.astype(jnp.bfloat16)
-    gate_out = jnp.dot(queries, gate_low, preferred_element_type=jnp.float32)
-    up_out = jnp.dot(queries, up_low, preferred_element_type=jnp.float32)
-    output = contract_columns((jax.nn.silu(gate_out) * up_out).astype(jnp.bfloat16), down_low)
-    return (rms_scale(output) * out_gain_row).astype(jnp.bfloat16), fresh
+    count = tokens.shape[0]
+    width, inner = fasts[0].shape
+    whole = pl.BlockSpec(memory_space=pltpu.VMEM)
+    results = pl.pallas_call(
+        update_kernel,
+        out_shape=[
+            jax.ShapeDtypeStruct(queries.shape, jnp.bfloat16),
+            *(jax.ShapeDtypeStruct(fast.shape, jnp.float32) for fast in fasts),
+        ],
+        in_specs=[whole] * 9,
+        out_specs=[whole] * 4,
+        scratch_shapes=[
+            pltpu.VMEM((3, width, inner), jnp.bfloat16),
+            pltpu.VMEM((width, count), jnp.bfloat16),
+            pltpu.VMEM((width, count), jnp.bfloat16),
+            pltpu.VMEM((3, count, inner), jnp.bfloat16),
+            pltpu.VMEM((3, width, inner), jnp.float32),
+            pltpu.VMEM((3, width, inner), jnp.bfloat16),
+        ],
+        compiler_params=pltpu.CompilerParams(vmem_limit_bytes=50 * 2**20),
+        cost_estimate=pl.CostEstimate(
+            flops=12 * count * width * inner + 12 * width * width * (2 * inner + width),
+            bytes_accessed=32 * width * inner,
+            transcendentals=count * inner,
+        ),
+        name="update",
+    )(tokens, queries, *fasts, *norms, out_gain_row)
+    return results[0], tuple(results[1:])
 
 
 def shards(stream, in_gain, w_qkv, qk_gain, w_one, w_three, w_two, token_rate, out_gain, w_out):
@@ -157,7 +228,7 @@
             prepared.append((queries, all_tokens(own)))
         fasts, results = initial, []
         for (queries, tokens), source in zip(prepared, sources):
-            normed_out, fasts = trained(tokens, queries, fasts, norms, out_gain[0, 0])
+            normed_out, fasts = trained(tokens, queries, fasts, norms, out_gain[0])
             head_terms = jnp.dot(normed_out, w_out[0, 0], preferred_element_type=jnp.float32)
             delta = summed_columns(head_terms, "head")
             results.append((source.astype(jnp.float32) + delta).astype(jnp.bfloat16))

time: 659 us -> 429 us (0.65)
  matrix products: 349 us -> 41.2 us
  Pallas kernels: 0 us -> 97.5 us
  between operations: 9.52 us -> 1.33 us
    dot_general x80 -> x0, matrix products: 298 us -> none  [the longest x24 97.6 us: orthogonal(): jnp.dot(mixing, current, preferred_element_type=jnp.float32)]
    pallas_call x0 -> x4, Pallas kernels: none -> 97.5 us  [trained(): pl.pallas_call(update_kernel, out_shape=[jax.ShapeDtypeStruct(queries.sha...]
    unnamed x153 -> x83, local copies, waits for them, and re-layouts: 42.9 us -> 54 us
    dot_general x4, matrix products: 15.2 us -> 5.87 us  [section(): jnp.dot(normed_out, w_out[0, 0], preferred_element_type=jnp.float32)]
    dynamic_update_slice x12, local copies, waits for them, and re-layouts: 13.9 us -> 6.39 us  [gathered_columns(): lax.dynamic_update_index_in_dim(whole, piece, (here - by) % devices, 1)]
  transfers between devices with their start and end apart: 58 -> 58, of which waited for: 31 -> 28; matrix products, arithmetic and copies ran while one was open for 42% -> 20% of each run, Pallas kernels for 0% -> 17%
where the time goes in v2:
time: 429 us; the launch traced here: 424 us
  Pallas kernels  97.5 us (23%)
  local copies, waits for them, and re-layouts  91.9 us (21%)
  waiting for transfers between devices  90.3 us (21%)
  starting transfers between devices  84.2 us (20%)
  matrix products  41.2 us (10%)
  other arithmetic  17.3 us (4%)
    pallas_call x4, Pallas kernels, trained(): pl.pallas_call(update_kernel, out_shape=[jax.ShapeDtypeStruct(queries.sha...  97.5 us
    ppermute x56, waiting for transfers between devices, turned(): lax.ppermute(array, axis, [(i, (i + by) % devices) for i in range(devices)])  86.4 us
    ppermute x56, starting transfers between devices, turned(): lax.ppermute(array, axis, [(i, (i + by) % devices) for i in range(devices)])  80.2 us
    unnamed x83, local copies, waits for them, and re-layouts  54 us
    dot_general x4, matrix products, project(): projected = jnp.dot(normed, qkv_matrix, preferred_element_type=jnp.float32)  35.4 us
    convert_element_type x6, local copies, waits for them, and re-layouts, project(): (rms_scale(whole.astype(jnp.float32)) * gain_row).astype(jnp.bfloat16)  10.3 us
  transfers between devices with their start and end apart: 58, of which 28 were waited for; matrix products, arithmetic and copies ran while one was open for 20% of the time, Pallas kernels for 17%

profile of v2, /device:TPU:1, one launch (start us, length us, event | category | flops | bytes accessed | tf_op | source)
XLA Modules:
  0.0 423.7 jit_solution(18395906442447266737)
XLA Ops:
  12.1 17.0 %copy.27 = bf16[1,4096,1,3,512]{1,4,3,2,0:T(8,128)(2,1)} copy(bf16[1,4096,1,3,512]{4,1,3,2,0:T(8,128)(2,1)} %param.12) | data formatting | bytes 25165824 | tf_op args[2]
  30.9 4.5 %collective-permute-done.31 = bf16[128,1024]{1,0:T(8,128)(2,1)S(1)} collective-permute-done((bf16[128,1024]{1,0:T(8,128)(2,1)}, bf16[128,1024]{1,0:T(8,128)(2,1)S(1)}, u32[]{:S(2)}, u32[]{:S(2)}) %collective-permute-start.31) | collective-permute-done | bytes 262176 | tf_op jit(solution)/shard_map/ppermute | solution.py:21
  40.7 8.8 %fusion.6 = f32[128,3,512]{2,0,1:T(8,128)S(1)} fusion(bf16[128,4096,1]{1,0,2:T(8,128)(2,1)S(1)} %reshape.230, bf16[1,4096,1,3,512]{1,4,3,2,0:T(8,128)(2,1)} %copy.27), kind=kOutput, calls=%fused_computation.6 | convolution fusion | flops 1610612736 | bytes 14417920 | tf_op jit(solution)/shard_map/dot_general | solution.py:76
  52.5 8.8 %fusion.2 = f32[128,3,512]{2,0,1:T(8,128)S(1)} fusion(bf16[128,4096,1]{1,0,2:T(8,128)(2,1)S(1)} %reshape.234, bf16[1,4096,1,3,512]{1,4,3,2,0:T(8,128)(2,1)} %copy.27), kind=kOutput, calls=%fused_computation.2 | convolution fusion | flops 1610612736 | bytes 14417920 | tf_op jit(solution)/shard_map/dot_general | solution.py:76
  91.2 4.2 collective-permute-start.10
  101.7 5.1 %collective-permute-done.35 = bf16[128,1024]{1,0:T(8,128)(2,1)S(1)} collective-permute-done((bf16[128,1024]{1,0:T(8,128)(2,1)S(1)}, bf16[128,1024]{1,0:T(8,128)(2,1)S(1)}, u32[]{:S(2)}, u32[]{:S(2)}) %collective-permute-start.35) | collective-permute-done | bytes 262176 | tf_op jit(solution)/shard_map/ppermute | solution.py:21
  107.7 4.5 %collective-permute-done.32 = bf16[128,1024]{1,0:T(8,128)(2,1)S(1)} collective-permute-done((bf16[128,1024]{1,0:T(8,128)(2,1)S(1)}, bf16[128,1024]{1,0:T(8,128)(2,1)S(1)}, u32[]{:S(2)}, u32[]{:S(2)}) %collective-permute-start.32) | collective-permute-done | bytes 262176 | tf_op jit(solution)/shard_map/ppermute | solution.py:21
  115.3 8.2 %collective-permute-done.36 = bf16[128,1024]{1,0:T(8,128)(2,1)S(1)} collective-permute-done((bf16[128,1024]{1,0:T(8,128)(2,1)S(1)}, bf16[128,1024]{1,0:T(8,128)(2,1)S(1)}, u32[]{:S(2)}, u32[]{:S(2)}) %collective-permute-start.36) | collective-permute-done | bytes 262176 | tf_op jit(solution)/shard_map/ppermute | solution.py:21
  129.1 6.5 %copy.44 = bf16[4096,512]{1,0:T(8,128)(2,1)} copy(bf16[4096,512]{0,1:T(8,128)(2,1)} %bitcast.261) | data formatting | bytes 8388608 | tf_op jit(solution)/shard_map/dot_general | solution.py:232
  142.7 24.4 %update.4 = (bf16[128,512]{1,0:T(8,128)(2,1)S(1)}, f32[512,768]{1,0:T(8,128)S(1)}, f32[512,768]{1,0:T(8,128)S(1)}, f32[512,768]{1,0:T(8,128)}) custom-call(bf16[2048,1024]{1,0:T(8,128)(2,1)} %copy-done.21, f32[128,512]{1,0:T(8,128)S(1)} %get-tuple-element.131.queries, f32[512,768]{1,0:T(8,128)} %get-tuple-element.142.gate, ...), custom_call_target="tpu_custom_call" | custom-call | flops 16106127360 | bytes 12582912 | tf_op jit(solution)/shard_map/update/pallas_call | solution.py:177
  167.1 4.3 %constant_dynamic-update-slice_fusion.42.tokens = bf16[2048,1024]{1,0:T(8,128)(2,1)} fusion(bf16[2048,1024]{1,0:T(8,128)(2,1)} %copy-done.25, bf16[1024,1024]{1,0:T(8,128)(2,1)} %collective-permute-done.39), kind=kLoop, calls=%fused_computation.180 | loop fusion | bytes 4194304 | tf_op jit(solution)/shard_map/concatenate | solution.py:57
  171.4 24.5 %update.6 = (bf16[128,512]{1,0:T(8,128)(2,1)S(1)}, f32[512,768]{1,0:T(8,128)}, f32[512,768]{1,0:T(8,128)}, f32[512,768]{1,0:T(8,128)}) custom-call(bf16[2048,1024]{1,0:T(8,128)(2,1)} %constant_dynamic-update-slice_fusion.42.tokens, f32[128,512]{1,0:T(8,128)S(1)} %get-tuple-element.54.queries, f32[512,768]{1,0:T(8,128)} %copy-done.3, f32[512,768]{1,0:T(8,128)} %copy-done.4, ...), custom_call_target="tpu_custom_call" | custom-call | flops 16106127360 | bytes 12582912 | tf_op jit(solution)/shard_map/update/pallas_call | solution.py:177
  207.6 5.4 %collective-permute-done.41 = bf16[128,1024]{1,0:T(8,128)(2,1)S(1)} collective-permute-done((bf16[128,1024]{1,0:T(8,128)(2,1)S(1)}, bf16[128,1024]{1,0:T(8,128)(2,1)S(1)}, u32[]{:S(2)}, u32[]{:S(2)}) %collective-permute-start.41) | collective-permute-done | bytes 262176 | tf_op jit(solution)/shard_map/ppermute | solution.py:21
  212.9 5.4 %collective-permute-done.11 = bf16[128,1024]{1,0:T(8,128)(2,1)S(1)} collective-permute-done((bf16[128,1024]{1,0:T(8,128)(2,1)S(1)}, bf16[128,1024]{1,0:T(8,128)(2,1)S(1)}, u32[]{:S(2)}, u32[]{:S(2)}) %collective-permute-start.11) | collective-permute-done | bytes 262176 | tf_op jit(solution)/shard_map/ppermute | solution.py:21
  218.4 5.8 %collective-permute-done.12 = bf16[128,1024]{1,0:T(8,128)(2,1)S(1)} collective-permute-done((bf16[128,1024]{1,0:T(8,128)(2,1)S(1)}, bf16[128,1024]{1,0:T(8,128)(2,1)S(1)}, u32[]{:S(2)}, u32[]{:S(2)}) %collective-permute-start.12) | collective-permute-done | bytes 262176 | tf_op jit(solution)/shard_map/ppermute | solution.py:21
  252.3 8.9 %fusion.4 = f32[128,3,512]{2,0,1:T(8,128)S(1)} fusion(bf16[128,4096,1]{1,0,2:T(8,128)(2,1)S(1)} %reshape.232, bf16[1,4096,1,3,512]{1,4,3,2,0:T(8,128)(2,1)} %copy.27), kind=kOutput, calls=%fused_computation.4 | convolution fusion | flops 1610612736 | bytes 14417920 | tf_op jit(solution)/shard_map/dot_general | solution.py:76
  271.3 8.8 %fusion = f32[128,3,512]{2,0,1:T(8,128)S(1)} fusion(bf16[128,4096,1]{1,0,2:T(8,128)(2,1)S(1)} %reshape.236, bf16[1,4096,1,3,512]{1,4,3,2,0:T(8,128)(2,1)} %copy.27), kind=kOutput, calls=%fused_computation | convolution fusion | flops 1610612736 | bytes 14417920 | tf_op jit(solution)/shard_map/dot_general | solution.py:76
  300.4 4.8 %collective-permute-done.23 = bf16[128,1024]{1,0:T(8,128)(2,1)S(1)} collective-permute-done((bf16[128,1024]{1,0:T(8,128)(2,1)S(1)}, bf16[128,1024]{1,0:T(8,128)(2,1)S(1)}, u32[]{:S(2)}, u32[]{:S(2)}) %collective-permute-start.23) | collective-permute-done | bytes 262176 | tf_op jit(solution)/shard_map/ppermute | solution.py:21
  306.7 6.2 %collective-permute-start.25 = (bf16[1024,1024]{1,0:T(8,128)(2,1)}, bf16[1024,1024]{1,0:T(8,128)(2,1)S(1)}, u32[]{:S(2)}, u32[]{:S(2)}) collective-permute-start(bf16[1024,1024]{1,0:T(8,128)(2,1)} %get-tuple-element.61), channel_id=1, source_target_pairs={{0,4},{4,0},{1,5},{5,1},{2,6},{6,2},{3,7},{7,3},{8,12},{12,8},{9,1... | collective-permute-start | bytes 6291464 | tf_op jit(solution)/shard_map/ppermute | solution.py:21
  317.4 4.9 %collective-permute-done.50 = bf16[128,1024]{1,0:T(8,128)(2,1)} collective-permute-done((bf16[128,1024]{1,0:T(8,128)(2,1)}, bf16[128,1024]{1,0:T(8,128)(2,1)}, u32[]{:S(2)}, u32[]{:S(2)}) %collective-permute-start.50) | collective-permute-done | bytes 262176 | tf_op jit(solution)/shard_map/ppermute | solution.py:21
  345.7 24.0 %update.5 = (bf16[128,512]{1,0:T(8,128)(2,1)S(1)}, f32[512,768]{1,0:T(8,128)S(1)}, f32[512,768]{1,0:T(8,128)S(1)}, f32[512,768]{1,0:T(8,128)}) custom-call(bf16[2048,1024]{1,0:T(8,128)(2,1)} %copy-done.24, f32[128,512]{1,0:T(8,128)S(1)} %get-tuple-element.134.queries, f32[512,768]{1,0:T(8,128)} %get-tuple-element.142.gate, ...), custom_call_target="tpu_custom_call" | custom-call | flops 16106127360 | bytes 12582912 | tf_op jit(solution)/shard_map/update/pallas_call | solution.py:177
  381.4 24.5 %update.7 = (bf16[128,512]{1,0:T(8,128)(2,1)S(1)}, f32[512,768]{1,0:T(8,128)}, f32[512,768]{1,0:T(8,128)}, f32[512,768]{1,0:T(8,128)}) custom-call(bf16[2048,1024]{1,0:T(8,128)(2,1)} %copy-done.19, f32[128,512]{1,0:T(8,128)S(1)} %get-tuple-element.48.queries, f32[512,768]{1,0:T(8,128)} %copy-done.1, f32[512,768]{1,0:T(8,128)} %copy-done.2, ...), custom_call_target="tpu_custom_call" | custom-call | flops 16106127360 | bytes 12582912 | tf_op jit(solution)/shard_map/update/pallas_call | solution.py:177
  410.9 6.2 %collective-permute-done.55 = bf16[128,1024]{1,0:T(8,128)(2,1)S(1)} collective-permute-done((bf16[128,1024]{1,0:T(8,128)(2,1)S(1)}, bf16[128,1024]{1,0:T(8,128)(2,1)S(1)}, u32[]{:S(2)}, u32[]{:S(2)}) %collective-permute-start.55) | collective-permute-done | bytes 262176 | tf_op jit(solution)/shard_map/ppermute | solution.py:21
  417.2 3.6 collective-permute-done.56
  (279 shorter events, 193.0 us)
Async XLA Ops:
  2.0 27.1 %collective-permute-start = (bf16[128,1024]{1,0:T(8,128)(2,1)}, bf16[128,1024]{1,0:T(8,128)(2,1)S(1)}, u32[]{:S(2)}, u32[]{:S(2)}) collective-permute-start(bf16[128,1024]{1,0:T(8,128)(2,1)} %get-tuple-element.59), channel_id=1, source_target_pairs={{0,1},{1,2},{2,3},{3,0},{4,5},{5,6},{6,7},{7,4},{8,9},{9,10},{10,1... | collective-permute-start | bytes 786440 | tf_op jit(solution)/shard_map/ppermute | solution.py:21
  4.4 26.4 %collective-permute-start.1 = (bf16[128,1024]{1,0:T(8,128)(2,1)}, bf16[128,1024]{1,0:T(8,128)(2,1)S(1)}, u32[]{:S(2)}, u32[]{:S(2)}) collective-permute-start(bf16[128,1024]{1,0:T(8,128)(2,1)} %get-tuple-element.59), channel_id=1, source_target_pairs={{0,2},{1,3},{2,0},{3,1},{4,6},{5,7},{6,4},{7,5},{8,10},{9,11},{10,... | collective-permute-start | bytes 786440 | tf_op jit(solution)/shard_map/ppermute | solution.py:21
  7.7 22.1 %collective-permute-start.29 = (bf16[128,1024]{1,0:T(8,128)(2,1)}, bf16[128,1024]{1,0:T(8,128)(2,1)}, u32[]{:S(2)}, u32[]{:S(2)}) collective-permute-start(bf16[128,1024]{1,0:T(8,128)(2,1)} %get-tuple-element.60), channel_id=1, source_target_pairs={{0,1},{1,2},{2,3},{3,0},{4,5},{5,6},{6,7},{7,4},{8,9},{9,10},{10,1... | collective-permute-start | bytes 786440 | tf_op jit(solution)/shard_map/ppermute | solution.py:21
  7.7 23.1 %collective-permute-start.30 = (bf16[128,1024]{1,0:T(8,128)(2,1)}, bf16[128,1024]{1,0:T(8,128)(2,1)S(1)}, u32[]{:S(2)}, u32[]{:S(2)}) collective-permute-start(bf16[128,1024]{1,0:T(8,128)(2,1)} %get-tuple-element.60), channel_id=1, source_target_pairs={{0,2},{1,3},{2,0},{3,1},{4,6},{5,7},{6,4},{7,5},{8,10},{9,11},{10,... | collective-permute-start | bytes 786440 | tf_op jit(solution)/shard_map/ppermute | solution.py:21
  9.6 21.3 %collective-permute-start.2 = (bf16[128,1024]{1,0:T(8,128)(2,1)}, bf16[128,1024]{1,0:T(8,128)(2,1)}, u32[]{:S(2)}, u32[]{:S(2)}) collective-permute-start(bf16[128,1024]{1,0:T(8,128)(2,1)} %get-tuple-element.59), channel_id=1, source_target_pairs={{0,3},{1,0},{2,1},{3,2},{4,7},{5,4},{6,5},{7,6},{8,11},{9,8},{10,9... | collective-permute-start | bytes 786440 | tf_op jit(solution)/shard_map/ppermute | solution.py:21
  70.9 15.3 %collective-permute-start.7 = (bf16[128,1024]{1,0:T(8,128)(2,1)S(1)}, bf16[128,1024]{1,0:T(8,128)(2,1)S(1)}, u32[]{:S(2)}, u32[]{:S(2)}) collective-permute-start(bf16[128,1024]{1,0:T(8,128)(2,1)S(1)} %collective-permute-done.6), channel_id=1, source_target_pairs={{0,8},{8,16},{16,24},{24,0},{1,9},{9,17},{17,25},{25,1},{2,10},{10... | collective-permute-start | bytes 786440 | tf_op jit(solution)/shard_map/ppermute | solution.py:21
  71.4 18.1 %collective-permute-start.8 = (bf16[128,1024]{1,0:T(8,128)(2,1)S(1)}, bf16[128,1024]{1,0:T(8,128)(2,1)S(1)}, u32[]{:S(2)}, u32[]{:S(2)}) collective-permute-start(bf16[128,1024]{1,0:T(8,128)(2,1)S(1)} %collective-permute-done.6), channel_id=1, source_target_pairs={{0,16},{8,24},{16,0},{24,8},{1,17},{9,25},{17,1},{25,9},{2,18},{10... | collective-permute-start | bytes 786440 | tf_op jit(solution)/shard_map/ppermute | solution.py:21
  73.5 16.8 %collective-permute-start.9 = (bf16[128,1024]{1,0:T(8,128)(2,1)S(1)}, bf16[128,1024]{1,0:T(8,128)(2,1)S(1)}, u32[]{:S(2)}, u32[]{:S(2)}) collective-permute-start(bf16[128,1024]{1,0:T(8,128)(2,1)S(1)} %collective-permute-done.6), channel_id=1, source_target_pairs={{0,24},{8,0},{16,8},{24,16},{1,25},{9,1},{17,9},{25,17},{2,26},{10... | collective-permute-start | bytes 786440 | tf_op jit(solution)/shard_map/ppermute | solution.py:21
  91.2 46.2 %collective-permute-start.10 = (bf16[1024,1024]{1,0:T(8,128)(2,1)}, bf16[1024,1024]{1,0:T(8,128)(2,1)}, u32[]{:S(2)}, u32[]{:S(2)}) collective-permute-start(bf16[1024,1024]{1,0:T(8,128)(2,1)} %get-tuple-element.95), channel_id=1, source_target_pairs={{0,4},{4,0},{1,5},{5,1},{2,6},{6,2},{3,7},{7,3},{8,12},{12,8},{9,1... | collective-permute-start | bytes 6291464 | tf_op jit(solution)/shard_map/ppermute | solution.py:21
  98.1 14.8 %collective-permute-start.33 = (bf16[128,1024]{1,0:T(8,128)(2,1)S(1)}, bf16[128,1024]{1,0:T(8,128)(2,1)S(1)}, u32[]{:S(2)}, u32[]{:S(2)}) collective-permute-start(bf16[128,1024]{1,0:T(8,128)(2,1)S(1)} %get-tuple-element.128), channel_id=1, source_target_pairs={{0,16},{8,24},{16,0},{24,8},{1,17},{9,25},{17,1},{25,9},{2,18},{10... | collective-permute-start | bytes 786440 | tf_op jit(solution)/shard_map/ppermute | solution.py:21
  106.8 16.7 %collective-permute-start.36 = (bf16[128,1024]{1,0:T(8,128)(2,1)S(1)}, bf16[128,1024]{1,0:T(8,128)(2,1)S(1)}, u32[]{:S(2)}, u32[]{:S(2)}) collective-permute-start(bf16[128,1024]{1,0:T(8,128)(2,1)S(1)} %collective-permute-done.35), channel_id=1, source_target_pairs={{0,8},{8,16},{16,24},{24,0},{1,9},{9,17},{17,25},{25,1},{2,10},{10... | collective-permute-start | bytes 786440 | tf_op jit(solution)/shard_map/ppermute | solution.py:21
  127.8 39.3 %collective-permute-start.39 = (bf16[1024,1024]{1,0:T(8,128)(2,1)}, bf16[1024,1024]{1,0:T(8,128)(2,1)}, u32[]{:S(2)}, u32[]{:S(2)}) collective-permute-start(bf16[1024,1024]{1,0:T(8,128)(2,1)} %get-tuple-element.112), channel_id=1, source_target_pairs={{0,4},{4,0},{1,5},{5,1},{2,6},{6,2},{3,7},{7,3},{8,12},{12,8},{9,1... | collective-permute-start | bytes 6291464 | tf_op jit(solution)/shard_map/ppermute | solution.py:21
  203.9 20.2 %collective-permute-start.12 = (bf16[128,1024]{1,0:T(8,128)(2,1)S(1)}, bf16[128,1024]{1,0:T(8,128)(2,1)S(1)}, u32[]{:S(2)}, u32[]{:S(2)}) collective-permute-start(bf16[128,1024]{1,0:T(8,128)(2,1)S(1)} %get-tuple-element.41), channel_id=1, source_target_pairs={{0,2},{1,3},{2,0},{3,1},{4,6},{5,7},{6,4},{7,5},{8,10},{9,11},{10,... | collective-permute-start | bytes 786440 | tf_op jit(solution)/shard_map/ppermute | solution.py:21
  207.0 17.2 %collective-permute-start.13 = (bf16[128,1024]{1,0:T(8,128)(2,1)S(1)}, bf16[128,1024]{1,0:T(8,128)(2,1)S(1)}, u32[]{:S(2)}, u32[]{:S(2)}) collective-permute-start(bf16[128,1024]{1,0:T(8,128)(2,1)S(1)} %get-tuple-element.40), channel_id=1, source_target_pairs={{0,3},{1,0},{2,1},{3,2},{4,7},{5,4},{6,5},{7,6},{8,11},{9,8},{10,9... | collective-permute-start | bytes 786440 | tf_op jit(solution)/shard_map/ppermute | solution.py:21
  237.5 23.8 %collective-permute-start.44 = (bf16[128,1024]{1,0:T(8,128)(2,1)S(1)}, bf16[128,1024]{1,0:T(8,128)(2,1)S(1)}, u32[]{:S(2)}, u32[]{:S(2)}) collective-permute-start(bf16[128,1024]{1,0:T(8,128)(2,1)S(1)} %collective-permute-done.43), channel_id=1, source_target_pairs={{0,1},{1,2},{2,3},{3,0},{4,5},{5,6},{6,7},{7,4},{8,9},{9,10},{10,1... | collective-permute-start | bytes 786440 | tf_op jit(solution)/shard_map/ppermute | solution.py:21
  240.0 21.3 %collective-permute-start.45 = (bf16[128,1024]{1,0:T(8,128)(2,1)S(1)}, bf16[128,1024]{1,0:T(8,128)(2,1)S(1)}, u32[]{:S(2)}, u32[]{:S(2)}) collective-permute-start(bf16[128,1024]{1,0:T(8,128)(2,1)S(1)} %collective-permute-done.43), channel_id=1, source_target_pairs={{0,2},{1,3},{2,0},{3,1},{4,6},{5,7},{6,4},{7,5},{8,10},{9,11},{10,... | collective-permute-start | bytes 786440 | tf_op jit(solution)/shard_map/ppermute | solution.py:21
  242.6 19.6 %collective-permute-start.46 = (bf16[128,1024]{1,0:T(8,128)(2,1)S(1)}, bf16[128,1024]{1,0:T(8,128)(2,1)S(1)}, u32[]{:S(2)}, u32[]{:S(2)}) collective-permute-start(bf16[128,1024]{1,0:T(8,128)(2,1)S(1)} %collective-permute-done.43), channel_id=1, source_target_pairs={{0,3},{1,0},{2,1},{3,2},{4,7},{5,4},{6,5},{7,6},{8,11},{9,8},{10,9... | collective-permute-start | bytes 786440 | tf_op jit(solution)/shard_map/ppermute | solution.py:21
  288.9 16.3 %collective-permute-start.23 = (bf16[128,1024]{1,0:T(8,128)(2,1)S(1)}, bf16[128,1024]{1,0:T(8,128)(2,1)S(1)}, u32[]{:S(2)}, u32[]{:S(2)}) collective-permute-start(bf16[128,1024]{1,0:T(8,128)(2,1)S(1)} %collective-permute-done.21), channel_id=1, source_target_pairs={{0,16},{8,24},{16,0},{24,8},{1,17},{9,25},{17,1},{25,9},{2,18},{10... | collective-permute-start | bytes 786440 | tf_op jit(solution)/shard_map/ppermute | solution.py:21
  306.7 36.8 %collective-permute-start.25 = (bf16[1024,1024]{1,0:T(8,128)(2,1)}, bf16[1024,1024]{1,0:T(8,128)(2,1)S(1)}, u32[]{:S(2)}, u32[]{:S(2)}) collective-permute-start(bf16[1024,1024]{1,0:T(8,128)(2,1)} %get-tuple-element.61), channel_id=1, source_target_pairs={{0,4},{4,0},{1,5},{5,1},{2,6},{6,2},{3,7},{7,3},{8,12},{12,8},{9,1... | collective-permute-start | bytes 6291464 | tf_op jit(solution)/shard_map/ppermute | solution.py:21
  322.4 16.9 %collective-permute-start.52 = (bf16[128,1024]{1,0:T(8,128)(2,1)}, bf16[128,1024]{1,0:T(8,128)(2,1)S(1)}, u32[]{:S(2)}, u32[]{:S(2)}) collective-permute-start(bf16[128,1024]{1,0:T(8,128)(2,1)} %collective-permute-done.50), channel_id=1, source_target_pairs={{0,16},{8,24},{16,0},{24,8},{1,17},{9,25},{17,1},{25,9},{2,18},{10... | collective-permute-start | bytes 786440 | tf_op jit(solution)/shard_map/ppermute | solution.py:21
  341.0 36.6 %collective-permute-start.54 = (bf16[1024,1024]{1,0:T(8,128)(2,1)}, bf16[1024,1024]{1,0:T(8,128)(2,1)}, u32[]{:S(2)}, u32[]{:S(2)}) collective-permute-start(bf16[1024,1024]{1,0:T(8,128)(2,1)} %get-tuple-element.78), channel_id=1, source_target_pairs={{0,4},{4,0},{1,5},{5,1},{2,6},{6,2},{3,7},{7,3},{8,12},{12,8},{9,1... | collective-permute-start | bytes 6291464 | tf_op jit(solution)/shard_map/ppermute | solution.py:21
  371.5 38.0 %collective-permute-start.26 = (bf16[128,1024]{1,0:T(8,128)(2,1)S(1)}, bf16[128,1024]{1,0:T(8,128)(2,1)S(1)}, u32[]{:S(2)}, u32[]{:S(2)}) collective-permute-start(bf16[128,1024]{1,0:T(8,128)(2,1)S(1)} %get-tuple-element.33), channel_id=1, source_target_pairs={{0,1},{1,2},{2,3},{3,0},{4,5},{5,6},{6,7},{7,4},{8,9},{9,10},{10,1... | collective-permute-start | bytes 786440 | tf_op jit(solution)/shard_map/ppermute | solution.py:21
  375.1 35.6 %collective-permute-start.27 = (bf16[128,1024]{1,0:T(8,128)(2,1)S(1)}, bf16[128,1024]{1,0:T(8,128)(2,1)S(1)}, u32[]{:S(2)}, u32[]{:S(2)}) collective-permute-start(bf16[128,1024]{1,0:T(8,128)(2,1)S(1)} %get-tuple-element.35), channel_id=1, source_target_pairs={{0,2},{1,3},{2,0},{3,1},{4,6},{5,7},{6,4},{7,5},{8,10},{9,11},{10,... | collective-permute-start | bytes 786440 | tf_op jit(solution)/shard_map/ppermute | solution.py:21
  376.7 34.0 %collective-permute-start.28 = (bf16[128,1024]{1,0:T(8,128)(2,1)S(1)}, bf16[128,1024]{1,0:T(8,128)(2,1)S(1)}, u32[]{:S(2)}, u32[]{:S(2)}) collective-permute-start(bf16[128,1024]{1,0:T(8,128)(2,1)S(1)} %get-tuple-element.34), channel_id=1, source_target_pairs={{0,3},{1,0},{2,1},{3,2},{4,7},{5,4},{6,5},{7,6},{8,11},{9,8},{10,9... | collective-permute-start | bytes 786440 | tf_op jit(solution)/shard_map/ppermute | solution.py:21
  (62 other events, 631.1 us)
